TPU v7x, 32 devices: a whole 2x2x4 slice. The times are simulated.
32 devices in a mesh: blk: 8 (over y, x, core), tp: 4 (over z).
Axes of the slice: x: 2, y: 2, z: 4, core: 2. Of those that a mesh axis runs over, the one named last changes fastest.
Arguments:
- text_emb: bfloat16 [12288, 1024], P('blk', 'tp'), may hold values from -4 to 4
- image_emb: bfloat16 [12288, 1024], P(('blk', 'tp')), may hold values from -4 to 4
- logit_scale: float32 [1], replicated, may hold values from 4 to 12
- logit_bias: float32 [1], replicated, may hold values from -3 to -1
- bucket: int32 [12288], replicated, may hold values from 0 to 3
- positive: int32 [12288], replicated, may hold values from 0 to 12287, as said below
- blocks: int32 [96, 8, 3], replicated, may hold values from -1 to 2, as said below
Outputs:
- text_grad: bfloat16 [12288, 1024], P('blk', 'tp')
- image_grad: bfloat16 [12288, 1024], P(('blk', 'tp'))
Inputs may be any that keep to these rules, and one draw needn't show every extreme that they name: positive[i] lies in the same 128-row tile as i, and within each tile the entries are a permutation of that tile's rows. `blocks`: each entry is a tile of the named shard or -1 for an unused slot; slot 0 is never -1; the used slots of one text tile and shard name different tiles; for the text tile's own blk index, slot 0 names the text tile's own tile.
All inputs are finite; a program needn't handle non-finite values.
Results may differ from a plain program's by a relative error of at most 0.015.
Values may be sent and summed in bfloat16 or wider, within the bound.
No kernel may reach another device: no remote copies, remote signals or barrier semaphores. Data moves between devices by JAX's collectives and lax.ppermute only.
A program may use at most 128 MiB of HBM per device.

v0:
```python
import jax
import jax.numpy as jnp
from jax import lax
from jax.sharding import PartitionSpec as P

TILE = 128
SLOTS = 3


def unit_rows(raw_rows):
    values = raw_rows.astype(jnp.float32)
    scales = lax.rsqrt(jnp.sum(values * values, axis=-1, keepdims=True) + 1e-06)
    return (values * scales, scales)


def grad_rows(raw_rows, scales, upstream):
    unit_float = raw_rows.astype(jnp.float32) * scales
    return (
        scales * (upstream - unit_float * jnp.sum(unit_float * upstream, axis=-1, keepdims=True))
    ).astype(jnp.bfloat16)


def pair_weights(
    text_part, text_ids, image_part, image_ids, live_mask, scale_value, bias_value, positive, bucket
):
    tile_rows = text_part.shape[1]
    products = jnp.einsum("cid,cjd->cij", text_part, image_part, preferred_element_type=jnp.float32)
    logits = scale_value * products + bias_value
    columns = image_ids[:, None] * tile_rows + jnp.arange(tile_rows, dtype=jnp.int32)[None, :]
    row_positive = positive.reshape(-1, tile_rows)[text_ids]
    row_bucket = bucket.reshape(-1, tile_rows)[text_ids]
    col_bucket = bucket.reshape(-1, tile_rows)[image_ids]
    matched = row_positive[:, :, None] == columns[:, None, :]
    labels = jnp.where(matched, 1.0, -1.0).astype(jnp.float32)
    kept_pairs = jnp.logical_or(matched, row_bucket[:, :, None] == col_bucket[:, None, :])
    pair_mask = (
        jnp.where(kept_pairs, 1.0, 0.0).astype(jnp.float32)
        * jnp.where(live_mask, 1.0, 0.0).astype(jnp.float32)[:, None, None]
    )
    return (scale_value * pair_mask * -labels * jax.nn.sigmoid(-labels * logits)).astype(
        jnp.bfloat16
    )


def per_device(text_emb, image_emb, logit_scale, logit_bias, bucket, positive, blocks):
    text_local = lax.all_to_all(text_emb, "tp", split_axis=0, concat_axis=1, tiled=True)
    text_float, text_scales = unit_rows(text_local)
    image_float, image_scales = unit_rows(image_emb)
    text_unit = text_float.astype(jnp.bfloat16)
    image_unit = image_float.astype(jnp.bfloat16)
    row_count = text_unit.shape[0]
    width = text_unit.shape[1]
    tile_count = row_count // TILE
    groups = lax.axis_size("tp")
    blk_index = lax.axis_index("blk")
    tp_index = lax.axis_index("tp")
    device = blk_index * groups + tp_index
    scale_value = logit_scale[0]
    bias_value = logit_bias[0]
    tile_range = jnp.arange(tile_count, dtype=jnp.int32)
    local_ids = device * tile_count + tile_range
    text_tiles = text_unit.reshape(tile_count, TILE, width)
    image_tiles = image_unit.reshape(tile_count, TILE, width)
    text_repeat = jnp.repeat(text_tiles, SLOTS, axis=0)
    text_ids = jnp.repeat(local_ids, SLOTS)
    own_blocks = lax.dynamic_slice_in_dim(blocks, device * tile_count, tile_count, 0)

    def listed_pairs(source, shard):
        listed = lax.dynamic_index_in_dim(own_blocks, source, 1, keepdims=False).reshape(-1)
        live_mask = listed >= 0
        local_tile = jnp.maximum(listed, 0)
        remote = shard.reshape(tile_count, TILE, width)[local_tile]
        remote_ids = (source * groups + tp_index) * tile_count + local_tile
        weights = pair_weights(
            text_repeat,
            text_ids,
            remote,
            remote_ids,
            live_mask,
            scale_value,
            bias_value,
            positive,
            bucket,
        )
        return (weights, remote, local_tile)

    def text_step(source, shard, text_acc):
        weights, remote, local_tile = listed_pairs(source, shard)
        update = jnp.einsum("cij,cjd->cid", weights, remote, preferred_element_type=jnp.float32)
        return text_acc + update.reshape(tile_count, SLOTS, TILE, width).sum(axis=1)

    def image_step(source, shard, image_acc):
        sender = source * groups + tp_index
        sender_blocks = lax.dynamic_slice_in_dim(blocks, sender * tile_count, tile_count, 0)
        listed = lax.dynamic_index_in_dim(sender_blocks, blk_index, 1, keepdims=False).reshape(-1)
        live_mask = listed >= 0
        local_tile = jnp.maximum(listed, 0)
        sender_text = jnp.repeat(shard.reshape(tile_count, TILE, width), SLOTS, axis=0)
        sender_ids = jnp.repeat(sender * tile_count + tile_range, SLOTS)
        mine = image_tiles[local_tile]
        weights = pair_weights(
            sender_text,
            sender_ids,
            mine,
            device * tile_count + local_tile,
            live_mask,
            scale_value,
            bias_value,
            positive,
            bucket,
        )
        update = jnp.einsum(
            "cij,cid->cjd", weights, sender_text, preferred_element_type=jnp.float32
        )
        return image_acc.at[local_tile].add(update)

    def over_shards(step_fn, piece, accum):
        count = piece.shape[0] // row_count

        def one_shard(offset, carried):
            shard = lax.dynamic_slice_in_dim(piece, offset * row_count, row_count, 0)
            return step_fn(offset, shard, carried)

        return lax.fori_loop(0, count, one_shard, accum)

    empty = jnp.zeros((tile_count, TILE, width), jnp.float32)
    text_acc = over_shards(text_step, lax.all_gather(image_unit, "blk", axis=0, tiled=True), empty)
    image_acc = over_shards(image_step, lax.all_gather(text_unit, "blk", axis=0, tiled=True), empty)
    text_grad_local = grad_rows(text_local, text_scales, text_acc.reshape(row_count, width))
    text_grad = lax.all_to_all(text_grad_local, "tp", split_axis=1, concat_axis=0, tiled=True)
    image_grad = grad_rows(image_emb, image_scales, image_acc.reshape(row_count, width))
    return (text_grad, image_grad)


def solution(mesh):
    in_specs = (P("blk", "tp"), P(("blk", "tp"), None), P(), P(), P(), P(), P())
    out_specs = (P("blk", "tp"), P(("blk", "tp"), None))
    return jax.shard_map(
        per_device, mesh=mesh, in_specs=in_specs, out_specs=out_specs, check_vma=False
    )
```

profile of v0, /device:TPU:0, one launch (start us, length us, event | category | flops | bytes accessed | tf_op | source)
XLA Modules:
  0.0 484.2 jit_solution(670990996590391568)
XLA Ops:
  10.8 6.4 %all-to-all-start = ((bf16[4,384,256]{2,1,0:T(8,128)(2,1)}), bf16[4,384,256]{2,1,0:T(8,128)(2,1)S(1)}, u32[]{:S(2)}, u32[]{:S(2)}) async-start(bf16[4,384,256]{2,1,0:T(8,128)(2,1)} %bitcast), calls=%async_computation | async-start | bytes 1572864 | tf_op jit(solution)/shard_map/all_to_all | solution.py:46
  18.2 19.1 %all-to-all-done = bf16[4,384,256]{2,1,0:T(8,128)(2,1)S(1)} async-done(((bf16[4,384,256]{2,1,0:T(8,128)(2,1)}), bf16[4,384,256]{2,1,0:T(8,128)(2,1)S(1)}, u32[]{:S(2)}, u32[]{:S(2)}) %all-to-all-start) | async-done | bytes 786464 | tf_op jit(solution)/shard_map/all_to_all | solution.py:46
  47.5 11.7 %all-gather.3.cloned.1.call-done = bf16[3072,1024]{1,0:T(8,128)(2,1)} async-done(((bf16[384,1024]{1,0:T(8,128)(2,1)}), bf16[3072,1024]{1,0:T(8,128)(2,1)}) %all-gather.3.cloned.1.call-update) | async-done | bytes 6291472 | tf_op jit(solution)/shard_map/all_gather | solution.py:127
  59.2 167.2 %while.34 = (s32[]{:T(128)}, f32[3,128,1024]{2,1,0:T(8,128)}, f32[]{:T(128)}, s32[9,128]{1,0:T(8,128)S(1)}, s32[]{:T(128)}, /*index=5*/s32[3,8,3]{2,0,1:T(4,128)...) while((s32[]{:T(128)}, f32[3,128,1024]{2,1,0:T(8,128)}, ...), condition=%wide.region_4.5_spmd.clone, body=%wide.region_2.4_spmd.clone.sunk | while | flops 608506112 | bytes 50346900 | solution.py:124
  65.8 2.9 broadcast_in_dim.267
  68.7 6.5 %fusion.96 = f32[9,128,1024]{2,1,0:T(8,128)} fusion(bf16[9,128,1024]{2,1,0:T(8,128)(2,1)S(1)} %gather_fusion.4, f32[9,128,128]{2,1,0:T(8,128)S(1)} %copy-done.5, bf16[9,128,1024]{2,1,0:T(8,128)(2,1)} %bitcast.122, f32[]{:T(128)} %get-tuple-element.975, f32[]{:T(128)} %get-tuple-element.969, pred[9,128,128]{2,1,0:T(32,128)(4,1)S(1)} %copy.32), kind=kOutput, calls=%fused_computation.68.clone.1 | convolution fusion | flops 605454336 | bytes 10174472 | tf_op jit(solution)/shard_map/while/body/eval_jaxpr/cij,cjd->cid/dot_general | solution.py:89
  75.3 3.1 reduce_sum.61
  86.7 2.9 broadcast_in_dim.267
  89.6 6.5 %fusion.96 = f32[9,128,1024]{2,1,0:T(8,128)} fusion(bf16[9,128,1024]{2,1,0:T(8,128)(2,1)S(1)} %gather_fusion.4, f32[9,128,128]{2,1,0:T(8,128)S(1)} %copy-done.5, bf16[9,128,1024]{2,1,0:T(8,128)(2,1)} %bitcast.122, f32[]{:T(128)} %get-tuple-element.975, f32[]{:T(128)} %get-tuple-element.969, pred[9,128,128]{2,1,0:T(32,128)(4,1)S(1)} %copy.32), kind=kOutput, calls=%fused_computation.68.clone.1 | convolution fusion | flops 605454336 | bytes 10174472 | tf_op jit(solution)/shard_map/while/body/eval_jaxpr/cij,cjd->cid/dot_general | solution.py:89
  96.2 3.2 reduce_sum.61
  107.7 2.9 broadcast_in_dim.267
  110.6 6.5 %fusion.96 = f32[9,128,1024]{2,1,0:T(8,128)} fusion(bf16[9,128,1024]{2,1,0:T(8,128)(2,1)S(1)} %gather_fusion.4, f32[9,128,128]{2,1,0:T(8,128)S(1)} %copy-done.5, bf16[9,128,1024]{2,1,0:T(8,128)(2,1)} %bitcast.122, f32[]{:T(128)} %get-tuple-element.975, f32[]{:T(128)} %get-tuple-element.969, pred[9,128,128]{2,1,0:T(32,128)(4,1)S(1)} %copy.32), kind=kOutput, calls=%fused_computation.68.clone.1 | convolution fusion | flops 605454336 | bytes 10174472 | tf_op jit(solution)/shard_map/while/body/eval_jaxpr/cij,cjd->cid/dot_general | solution.py:89
  117.2 3.1 reduce_sum.61
  128.6 2.9 broadcast_in_dim.267
  131.5 6.5 %fusion.96 = f32[9,128,1024]{2,1,0:T(8,128)} fusion(bf16[9,128,1024]{2,1,0:T(8,128)(2,1)S(1)} %gather_fusion.4, f32[9,128,128]{2,1,0:T(8,128)S(1)} %copy-done.5, bf16[9,128,1024]{2,1,0:T(8,128)(2,1)} %bitcast.122, f32[]{:T(128)} %get-tuple-element.975, f32[]{:T(128)} %get-tuple-element.969, pred[9,128,128]{2,1,0:T(32,128)(4,1)S(1)} %copy.32), kind=kOutput, calls=%fused_computation.68.clone.1 | convolution fusion | flops 605454336 | bytes 10174472 | tf_op jit(solution)/shard_map/while/body/eval_jaxpr/cij,cjd->cid/dot_general | solution.py:89
  138.0 3.1 reduce_sum.61
  149.5 2.9 broadcast_in_dim.267
  152.4 6.5 %fusion.96 = f32[9,128,1024]{2,1,0:T(8,128)} fusion(bf16[9,128,1024]{2,1,0:T(8,128)(2,1)S(1)} %gather_fusion.4, f32[9,128,128]{2,1,0:T(8,128)S(1)} %copy-done.5, bf16[9,128,1024]{2,1,0:T(8,128)(2,1)} %bitcast.122, f32[]{:T(128)} %get-tuple-element.975, f32[]{:T(128)} %get-tuple-element.969, pred[9,128,128]{2,1,0:T(32,128)(4,1)S(1)} %copy.32), kind=kOutput, calls=%fused_computation.68.clone.1 | convolution fusion | flops 605454336 | bytes 10174472 | tf_op jit(solution)/shard_map/while/body/eval_jaxpr/cij,cjd->cid/dot_general | solution.py:89
  158.9 3.1 reduce_sum.61
  170.4 2.9 broadcast_in_dim.267
  173.3 6.5 %fusion.96 = f32[9,128,1024]{2,1,0:T(8,128)} fusion(bf16[9,128,1024]{2,1,0:T(8,128)(2,1)S(1)} %gather_fusion.4, f32[9,128,128]{2,1,0:T(8,128)S(1)} %copy-done.5, bf16[9,128,1024]{2,1,0:T(8,128)(2,1)} %bitcast.122, f32[]{:T(128)} %get-tuple-element.975, f32[]{:T(128)} %get-tuple-element.969, pred[9,128,128]{2,1,0:T(32,128)(4,1)S(1)} %copy.32), kind=kOutput, calls=%fused_computation.68.clone.1 | convolution fusion | flops 605454336 | bytes 10174472 | tf_op jit(solution)/shard_map/while/body/eval_jaxpr/cij,cjd->cid/dot_general | solution.py:89
  179.8 3.1 reduce_sum.61
  191.3 2.9 broadcast_in_dim.267
  194.2 6.5 %fusion.96 = f32[9,128,1024]{2,1,0:T(8,128)} fusion(bf16[9,128,1024]{2,1,0:T(8,128)(2,1)S(1)} %gather_fusion.4, f32[9,128,128]{2,1,0:T(8,128)S(1)} %copy-done.5, bf16[9,128,1024]{2,1,0:T(8,128)(2,1)} %bitcast.122, f32[]{:T(128)} %get-tuple-element.975, f32[]{:T(128)} %get-tuple-element.969, pred[9,128,128]{2,1,0:T(32,128)(4,1)S(1)} %copy.32), kind=kOutput, calls=%fused_computation.68.clone.1 | convolution fusion | flops 605454336 | bytes 10174472 | tf_op jit(solution)/shard_map/while/body/eval_jaxpr/cij,cjd->cid/dot_general | solution.py:89
  200.7 3.1 reduce_sum.61
  212.2 2.9 broadcast_in_dim.267
  215.1 6.5 %fusion.96 = f32[9,128,1024]{2,1,0:T(8,128)} fusion(bf16[9,128,1024]{2,1,0:T(8,128)(2,1)S(1)} %gather_fusion.4, f32[9,128,128]{2,1,0:T(8,128)S(1)} %copy-done.5, bf16[9,128,1024]{2,1,0:T(8,128)(2,1)} %bitcast.122, f32[]{:T(128)} %get-tuple-element.975, f32[]{:T(128)} %get-tuple-element.969, pred[9,128,128]{2,1,0:T(32,128)(4,1)S(1)} %copy.32), kind=kOutput, calls=%fused_computation.68.clone.1 | convolution fusion | flops 605454336 | bytes 10174472 | tf_op jit(solution)/shard_map/while/body/eval_jaxpr/cij,cjd->cid/dot_general | solution.py:89
  221.6 3.1 reduce_sum.61
  226.4 3.0 reshape.452
  232.5 4.8 all-to-all-start.1
  237.3 20.5 %all-to-all-done.1 = bf16[384,4,256]{2,0,1:T(8,128)(2,1)S(1)} async-done(((bf16[384,4,256]{2,0,1:T(8,128)(2,1)}), bf16[384,4,256]{2,0,1:T(8,128)(2,1)S(1)}, u32[]{:S(2)}, u32[]{:S(2)}) %all-to-all-start.1) | async-done | bytes 786464 | tf_op jit(solution)/shard_map/all_to_all | solution.py:130
  259.2 213.7 %while.33 = (s32[]{:T(128)}, f32[3,128,1024]{2,1,0:T(8,128)}, s32[]{:T(128)}, s32[96,8,3]{2,0,1:T(8,128)}, s32[]{:T(128)}, /*index=5*/f32[]{:T(128)}, s32[12288]...) while((s32[]{:T(128)}, f32[3,128,1024]{2,1,0:T(8,128)}, ...), condition=%wide.region_8.9_spmd.clone, body=%wide.region_6.8_spmd.clone.sunk | while | flops 607670528 | bytes 33094608 | solution.py:124
  266.8 6.8 %fusion.91 = f32[9,128,1024]{2,1,0:T(8,128)} fusion(bf16[9,128,1024]{2,1,0:T(8,128)(2,1)S(1)} %bitcast.119, bf16[9,128,1024]{2,1,0:T(8,128)(2,1)} %gather_fusion, f32[]{:T(128)} %get-tuple-element.1036, f32[9]{0:T(128)S(1)} %select_n.297, s32[9,128]{1,0:T(8,128)S(1)} %gather_fusion.1, s32[9,128]{1,0:T(8,128)S(1)} %gather_fusion.2, ...), kind=kOutput, calls=%fused_computation.21.clone.1 | convolution fusion | flops 606486528 | bytes 9455660 | tf_op jit(solution)/shard_map/while/body/eval_jaxpr/cij,cid->cjd/dot_general | solution.py:112
  273.6 12.4 %scatter_fusion = f32[3,128,1024]{2,1,0:T(8,128)} fusion(f32[3,128,1024]{2,1,0:T(8,128)} %get-tuple-element.1006, s32[9]{0:T(128)S(1)} %reshape.610, f32[9,128,1024]{2,1,0:T(8,128)} %fusion.91), kind=kCustom, calls=%fused_computation.8.clone.clone.1 | custom fusion | flops 1179648 | bytes 14155812 | tf_op jit(solution)/shard_map/while/body/eval_jaxpr/scatter-add | solution.py:115
  293.5 6.8 %fusion.91 = f32[9,128,1024]{2,1,0:T(8,128)} fusion(bf16[9,128,1024]{2,1,0:T(8,128)(2,1)S(1)} %bitcast.119, bf16[9,128,1024]{2,1,0:T(8,128)(2,1)} %gather_fusion, f32[]{:T(128)} %get-tuple-element.1036, f32[9]{0:T(128)S(1)} %select_n.297, s32[9,128]{1,0:T(8,128)S(1)} %gather_fusion.1, s32[9,128]{1,0:T(8,128)S(1)} %gather_fusion.2, ...), kind=kOutput, calls=%fused_computation.21.clone.1 | convolution fusion | flops 606486528 | bytes 9455660 | tf_op jit(solution)/shard_map/while/body/eval_jaxpr/cij,cid->cjd/dot_general | solution.py:112
  300.4 12.3 %scatter_fusion = f32[3,128,1024]{2,1,0:T(8,128)} fusion(f32[3,128,1024]{2,1,0:T(8,128)} %get-tuple-element.1006, s32[9]{0:T(128)S(1)} %reshape.610, f32[9,128,1024]{2,1,0:T(8,128)} %fusion.91), kind=kCustom, calls=%fused_computation.8.clone.clone.1 | custom fusion | flops 1179648 | bytes 14155812 | tf_op jit(solution)/shard_map/while/body/eval_jaxpr/scatter-add | solution.py:115
  320.2 6.8 %fusion.91 = f32[9,128,1024]{2,1,0:T(8,128)} fusion(bf16[9,128,1024]{2,1,0:T(8,128)(2,1)S(1)} %bitcast.119, bf16[9,128,1024]{2,1,0:T(8,128)(2,1)} %gather_fusion, f32[]{:T(128)} %get-tuple-element.1036, f32[9]{0:T(128)S(1)} %select_n.297, s32[9,128]{1,0:T(8,128)S(1)} %gather_fusion.1, s32[9,128]{1,0:T(8,128)S(1)} %gather_fusion.2, ...), kind=kOutput, calls=%fused_computation.21.clone.1 | convolution fusion | flops 606486528 | bytes 9455660 | tf_op jit(solution)/shard_map/while/body/eval_jaxpr/cij,cid->cjd/dot_general | solution.py:112
  327.1 12.4 %scatter_fusion = f32[3,128,1024]{2,1,0:T(8,128)} fusion(f32[3,128,1024]{2,1,0:T(8,128)} %get-tuple-element.1006, s32[9]{0:T(128)S(1)} %reshape.610, f32[9,128,1024]{2,1,0:T(8,128)} %fusion.91), kind=kCustom, calls=%fused_computation.8.clone.clone.1 | custom fusion | flops 1179648 | bytes 14155812 | tf_op jit(solution)/shard_map/while/body/eval_jaxpr/scatter-add | solution.py:115
  347.1 6.8 %fusion.91 = f32[9,128,1024]{2,1,0:T(8,128)} fusion(bf16[9,128,1024]{2,1,0:T(8,128)(2,1)S(1)} %bitcast.119, bf16[9,128,1024]{2,1,0:T(8,128)(2,1)} %gather_fusion, f32[]{:T(128)} %get-tuple-element.1036, f32[9]{0:T(128)S(1)} %select_n.297, s32[9,128]{1,0:T(8,128)S(1)} %gather_fusion.1, s32[9,128]{1,0:T(8,128)S(1)} %gather_fusion.2, ...), kind=kOutput, calls=%fused_computation.21.clone.1 | convolution fusion | flops 606486528 | bytes 9455660 | tf_op jit(solution)/shard_map/while/body/eval_jaxpr/cij,cid->cjd/dot_general | solution.py:112
  353.9 12.3 %scatter_fusion = f32[3,128,1024]{2,1,0:T(8,128)} fusion(f32[3,128,1024]{2,1,0:T(8,128)} %get-tuple-element.1006, s32[9]{0:T(128)S(1)} %reshape.610, f32[9,128,1024]{2,1,0:T(8,128)} %fusion.91), kind=kCustom, calls=%fused_computation.8.clone.clone.1 | custom fusion | flops 1179648 | bytes 14155812 | tf_op jit(solution)/shard_map/while/body/eval_jaxpr/scatter-add | solution.py:115
  373.7 6.8 %fusion.91 = f32[9,128,1024]{2,1,0:T(8,128)} fusion(bf16[9,128,1024]{2,1,0:T(8,128)(2,1)S(1)} %bitcast.119, bf16[9,128,1024]{2,1,0:T(8,128)(2,1)} %gather_fusion, f32[]{:T(128)} %get-tuple-element.1036, f32[9]{0:T(128)S(1)} %select_n.297, s32[9,128]{1,0:T(8,128)S(1)} %gather_fusion.1, s32[9,128]{1,0:T(8,128)S(1)} %gather_fusion.2, ...), kind=kOutput, calls=%fused_computation.21.clone.1 | convolution fusion | flops 606486528 | bytes 9455660 | tf_op jit(solution)/shard_map/while/body/eval_jaxpr/cij,cid->cjd/dot_general | solution.py:112
  380.6 12.2 %scatter_fusion = f32[3,128,1024]{2,1,0:T(8,128)} fusion(f32[3,128,1024]{2,1,0:T(8,128)} %get-tuple-element.1006, s32[9]{0:T(128)S(1)} %reshape.610, f32[9,128,1024]{2,1,0:T(8,128)} %fusion.91), kind=kCustom, calls=%fused_computation.8.clone.clone.1 | custom fusion | flops 1179648 | bytes 14155812 | tf_op jit(solution)/shard_map/while/body/eval_jaxpr/scatter-add | solution.py:115
  400.3 6.8 %fusion.91 = f32[9,128,1024]{2,1,0:T(8,128)} fusion(bf16[9,128,1024]{2,1,0:T(8,128)(2,1)S(1)} %bitcast.119, bf16[9,128,1024]{2,1,0:T(8,128)(2,1)} %gather_fusion, f32[]{:T(128)} %get-tuple-element.1036, f32[9]{0:T(128)S(1)} %select_n.297, s32[9,128]{1,0:T(8,128)S(1)} %gather_fusion.1, s32[9,128]{1,0:T(8,128)S(1)} %gather_fusion.2, ...), kind=kOutput, calls=%fused_computation.21.clone.1 | convolution fusion | flops 606486528 | bytes 9455660 | tf_op jit(solution)/shard_map/while/body/eval_jaxpr/cij,cid->cjd/dot_general | solution.py:112
  407.1 12.5 %scatter_fusion = f32[3,128,1024]{2,1,0:T(8,128)} fusion(f32[3,128,1024]{2,1,0:T(8,128)} %get-tuple-element.1006, s32[9]{0:T(128)S(1)} %reshape.610, f32[9,128,1024]{2,1,0:T(8,128)} %fusion.91), kind=kCustom, calls=%fused_computation.8.clone.clone.1 | custom fusion | flops 1179648 | bytes 14155812 | tf_op jit(solution)/shard_map/while/body/eval_jaxpr/scatter-add | solution.py:115
  427.2 6.8 %fusion.91 = f32[9,128,1024]{2,1,0:T(8,128)} fusion(bf16[9,128,1024]{2,1,0:T(8,128)(2,1)S(1)} %bitcast.119, bf16[9,128,1024]{2,1,0:T(8,128)(2,1)} %gather_fusion, f32[]{:T(128)} %get-tuple-element.1036, f32[9]{0:T(128)S(1)} %select_n.297, s32[9,128]{1,0:T(8,128)S(1)} %gather_fusion.1, s32[9,128]{1,0:T(8,128)S(1)} %gather_fusion.2, ...), kind=kOutput, calls=%fused_computation.21.clone.1 | convolution fusion | flops 606486528 | bytes 9455660 | tf_op jit(solution)/shard_map/while/body/eval_jaxpr/cij,cid->cjd/dot_general | solution.py:112
  434.0 12.2 %scatter_fusion = f32[3,128,1024]{2,1,0:T(8,128)} fusion(f32[3,128,1024]{2,1,0:T(8,128)} %get-tuple-element.1006, s32[9]{0:T(128)S(1)} %reshape.610, f32[9,128,1024]{2,1,0:T(8,128)} %fusion.91), kind=kCustom, calls=%fused_computation.8.clone.clone.1 | custom fusion | flops 1179648 | bytes 14155812 | tf_op jit(solution)/shard_map/while/body/eval_jaxpr/scatter-add | solution.py:115
  453.8 6.8 %fusion.91 = f32[9,128,1024]{2,1,0:T(8,128)} fusion(bf16[9,128,1024]{2,1,0:T(8,128)(2,1)S(1)} %bitcast.119, bf16[9,128,1024]{2,1,0:T(8,128)(2,1)} %gather_fusion, f32[]{:T(128)} %get-tuple-element.1036, f32[9]{0:T(128)S(1)} %select_n.297, s32[9,128]{1,0:T(8,128)S(1)} %gather_fusion.1, s32[9,128]{1,0:T(8,128)S(1)} %gather_fusion.2, ...), kind=kOutput, calls=%fused_computation.21.clone.1 | convolution fusion | flops 606486528 | bytes 9455660 | tf_op jit(solution)/shard_map/while/body/eval_jaxpr/cij,cid->cjd/dot_general | solution.py:112
  460.6 12.3 %scatter_fusion = f32[3,128,1024]{2,1,0:T(8,128)} fusion(f32[3,128,1024]{2,1,0:T(8,128)} %get-tuple-element.1006, s32[9]{0:T(128)S(1)} %reshape.610, f32[9,128,1024]{2,1,0:T(8,128)} %fusion.91), kind=kCustom, calls=%fused_computation.8.clone.clone.1 | custom fusion | flops 1179648 | bytes 14155812 | tf_op jit(solution)/shard_map/while/body/eval_jaxpr/scatter-add | solution.py:115
  (461 shorter events, 149.7 us)
Async XLA Ops:
  7.2 52.0 %all-gather.3.cloned.1.call-start = ((), (), s32[]{:S(2)}) async-start(), calls=%async_computation.2 | async-start | bytes 7077888 | tf_op jit(solution)/shard_map/all_gather | solution.py:127
  10.8 6.4 %copy-start.17 = (s32[96,8,3]{0,1,2:T(8,128)S(1)}, s32[96,8,3]{0,1,2:T(8,128)}, u32[]{:S(2)}) copy-start(s32[96,8,3]{0,1,2:T(8,128)} %param.17) | copy-start | bytes 27652
  10.8 6.8 %copy-start.15 = (s32[12288]{0:T(1024)S(1)}, s32[12288]{0:T(1024)}, u32[]{:S(2)}) copy-start(s32[12288]{0:T(1024)} %param.16) | copy-start | bytes 147460
  10.8 26.4 %all-to-all-start = ((bf16[4,384,256]{2,1,0:T(8,128)(2,1)}), bf16[4,384,256]{2,1,0:T(8,128)(2,1)S(1)}, u32[]{:S(2)}, u32[]{:S(2)}) async-start(bf16[4,384,256]{2,1,0:T(8,128)(2,1)} %bitcast), calls=%async_computation | async-start | bytes 1572864 | tf_op jit(solution)/shard_map/all_to_all | solution.py:46
  17.2 240.6 %all-gather.5.cloned.1.call-start = ((), (), s32[]{:S(2)}) async-start(), calls=%async_computation.3 | async-start | bytes 7077888 | tf_op jit(solution)/shard_map/all_gather | solution.py:128
  17.4 21.3 %copy-start.16 = (s32[96,8,3]{2,0,1:T(8,128)}, s32[96,8,3]{2,0,1:T(8,128)S(1)}, u32[]{:S(2)}) copy-start(s32[96,8,3]{2,0,1:T(8,128)S(1)} %copy.22) | copy-start | bytes 27652
  37.3 7.9 %copy-start.10 = (bf16[4,384,256]{2,1,0:T(8,128)(2,1)}, bf16[4,384,256]{2,1,0:T(8,128)(2,1)S(1)}, u32[]{:S(2)}) copy-start(bf16[4,384,256]{2,1,0:T(8,128)(2,1)S(1)} %all-to-all-done) | copy-start | bytes 2359300
  42.9 2.4 copy-start.7
  46.4 12.8 %copy-start.6 = (s32[12288]{0:T(1024)S(1)}, s32[12288]{0:T(1024)}, u32[]{:S(2)}) copy-start(s32[12288]{0:T(1024)} %param.15) | copy-start | bytes 147460
  65.8 2.9 copy-start.5
  75.3 3.1 copy-start.2
  79.0 1.2 copy-start.3
  86.7 2.9 copy-start.5
  96.2 3.2 copy-start.2
  99.9 1.2 copy-start.3
  107.7 2.9 copy-start.5
  117.2 3.1 copy-start.2
  120.8 1.2 copy-start.3
  128.6 2.9 copy-start.5
  138.0 3.1 copy-start.2
  141.7 1.2 copy-start.3
  149.5 2.9 copy-start.5
  158.9 3.1 copy-start.2
  162.6 1.2 copy-start.3
  170.4 2.9 copy-start.5
  179.8 3.1 copy-start.2
  183.5 1.2 copy-start.3
  191.3 2.9 copy-start.5
  200.7 3.1 copy-start.2
  204.4 1.2 copy-start.3
  212.1 2.9 copy-start.5
  221.6 3.1 copy-start.2
  225.3 1.2 copy-start.3
  226.4 3.0 copy-start.4
  226.4 3.0 copy-start.8
  229.5 1.1 copy-start.11
  229.5 1.7 copy-start.12
  232.5 26.7 %copy-start.1 = (bf16[384,1024]{1,0:T(8,128)(2,1)S(1)}, bf16[384,1024]{1,0:T(8,128)(2,1)}, u32[]{:S(2)}) copy-start(bf16[384,1024]{1,0:T(8,128)(2,1)} %fusion.57) | copy-start | bytes 2359300
  232.5 25.3 %all-to-all-start.1 = ((bf16[384,4,256]{2,0,1:T(8,128)(2,1)}), bf16[384,4,256]{2,0,1:T(8,128)(2,1)S(1)}, u32[]{:S(2)}, u32[]{:S(2)}) async-start(bf16[384,4,256]{2,0,1:T(8,128)(2,1)} %fusion.68), calls=%async_computation.1 | async-start | bytes 1572864 | tf_op jit(solution)/shard_map/all_to_all | solution.py:130
  257.8 1.4 copy-start.13
  472.9 2.2 copy-start
  472.9 2.3 copy-start.9
  475.2 1.2 copy-start.14
Sparse Core Ops, SparseCore 0:
  10.9 48.2 all-gather.2
  61.1 45.5 all-gather.4
where the time goes:
time: 488 us; the launch traced here: 484 us
  other arithmetic  164 us (34%)
  local copies, waits for them, and re-layouts  135 us (28%)
  matrix products  107 us (22%)
  waiting for transfers between devices  51.4 us (11%)
  between operations  14.1 us (3%)
  starting transfers between devices  11.2 us (2%)
    scatter-add x8, other arithmetic, image_step(): return image_acc.at[local_tile].add(update)  98.4 us
    dot_general x8, matrix products, image_step(): jnp.einsum('cij,cid->cjd', weights, sender_text, preferred_element_type=j...  54.7 us
    dot_general x8, matrix products, text_step(): jnp.einsum('cij,cjd->cid', weights, remote, preferred_element_type=jnp.fl...  52.2 us
    reduce_sum x8, other arithmetic, text_step(): return text_acc + update.reshape(tile_count, SLOTS, TILE, width).sum(axis=1)  24.9 us
    broadcast_in_dim x8, local copies, waits for them, and re-layouts, per_device(): text_repeat = jnp.repeat(text_tiles, SLOTS, axis=0)  23.3 us
    all_to_all x1, waiting for transfers between devices, per_device(): lax.all_to_all(text_grad_local, 'tp', split_axis=1, concat_axis=0, tiled=...  20.5 us
    all_to_all x1, waiting for transfers between devices, per_device(): lax.all_to_all(text_emb, 'tp', split_axis=0, concat_axis=1, tiled=True)  19.1 us
    gather x8, local copies, waits for them, and re-layouts, image_step(): mine = image_tiles[local_tile]  19.1 us
  transfers between devices with their start and end apart: 4, of which 3 were waited for; matrix products, arithmetic and copies ran while one was open for 36% of the time, Pallas kernels for 0%

commit v1 on v0

v1 whole, which is shorter than its diff:
```python
import functools
import math

import jax
import jax.numpy as jnp
from jax import lax
from jax.experimental import pallas as pl
from jax.experimental.pallas import tpu as pltpu
from jax.sharding import PartitionSpec as P

TILE = 128
SLOTS = 3
CORES = 2
EPS = 1e-06
LOG2E = math.log2(math.e)
VMEM_LIMIT = 56 * 1024 * 1024

VMEM_SPEC = pl.BlockSpec(memory_space=pltpu.VMEM)
SMEM_SPEC = pl.BlockSpec(memory_space=pltpu.SMEM)


def call_kernel(body, outs, operands, specs, scratch=(), flops=0, transcendentals=0):
    moved = sum(x.size * x.dtype.itemsize for x in operands)
    moved += sum(math.prod(o.shape) * o.dtype.itemsize for o in outs)
    return pl.pallas_call(
        body,
        out_shape=outs,
        in_specs=specs,
        out_specs=[VMEM_SPEC] * len(outs),
        scratch_shapes=list(scratch),
        compiler_params=pltpu.CompilerParams(vmem_limit_bytes=VMEM_LIMIT),
        cost_estimate=pl.CostEstimate(
            flops=flops, bytes_accessed=moved, transcendentals=transcendentals
        ),
    )(*operands)


def struct(shape, dtype):
    return jax.ShapeDtypeStruct(shape, dtype)


def row_scales(square_sum):
    return lax.rsqrt(square_sum + EPS)


def column_of(row):
    return jnp.broadcast_to(row, (TILE, TILE)).T


def weights_body(tile_count, chunks, piece_rows, own_pieces, *refs):
    piece_count = len(piece_rows)
    scale_ref, bias_ref, own_ref, other_ref = refs[:4]
    piece_refs = refs[4 : 4 + piece_count]
    rowb_ref, pos_ref, colb_ref, colid_ref = refs[4 + piece_count : 8 + piece_count]
    unit_ref, weight_ref, acc_own_ref, acc_other_ref, image_ref, acc_ref = refs[8 + piece_count :]
    rows = tile_count * TILE
    width = own_ref.shape[2]
    for half, source in enumerate((own_ref, other_ref)):
        for tile in range(tile_count):
            part = pl.ds(tile * TILE, TILE)
            parts = [source[c, part, :].astype(jnp.float32) for c in range(chunks)]
            total = sum(jnp.sum(x * x, axis=-1, keepdims=True) for x in parts)
            scales = row_scales(total)
            for c in range(chunks):
                unit_ref[pl.ds(half * rows + tile * TILE, TILE), pl.ds(c * width, width)] = (
                    parts[c] * scales
                ).astype(jnp.bfloat16)
    start = 0
    step = 64
    for piece, count in zip(piece_refs, piece_rows):
        for first in range(0, count, step):
            values = piece[pl.ds(first, step), :].astype(jnp.float32)
            scales = row_scales(jnp.sum(values * values, axis=-1, keepdims=True))
            image_ref[pl.ds(start + first, step), :] = (values * scales).astype(jnp.bfloat16)
        start += count
    scale = scale_ref[0]
    slope = -scale * LOG2E
    offset = -bias_ref[0] * LOG2E
    group = tile_count * TILE
    groups = start // group
    for q in range(groups):
        columns = pl.ds(q * group, group)
        images = image_ref[columns, :]
        products = lax.dot_general(
            unit_ref[...], images, (((1,), (1,)), ((), ())), preferred_element_type=jnp.float32
        )
        powers = products * slope + offset
        for a in range(2 * tile_count):
            row_bucket = column_of(rowb_ref[pl.ds(a, 1), :])
            for j in range(tile_count):
                lanes = pl.ds(q * group + j * TILE, TILE)
                power = powers[a * TILE : (a + 1) * TILE, j * TILE : (j + 1) * TILE]
                kept = row_bucket == colb_ref[pl.ds(a, 1), lanes]
                if a < tile_count and q in own_pieces:
                    matched = column_of(pos_ref[pl.ds(a, 1), :]) == colid_ref[:, lanes]
                    power = jnp.where(matched, -power, power)
                    factor = jnp.where(matched, -scale, jnp.where(kept, scale, 0.0))
                else:
                    factor = jnp.where(kept, scale, 0.0)
                weight_ref[pl.ds(a * TILE, TILE), lanes] = (
                    factor / (1.0 + jnp.exp2(power))
                ).astype(jnp.bfloat16)
        update = jnp.dot(weight_ref[:, columns], images, preferred_element_type=jnp.float32)
        if q == 0:
            acc_ref[...] = update
        else:
            acc_ref[...] += update
    acc_own_ref[...] = acc_ref[:rows, :]
    acc_other_ref[...] = acc_ref[rows:, :].astype(jnp.bfloat16)


def image_sum(weight_ref, unit_ref, columns):
    return lax.dot_general(
        weight_ref[:, columns],
        unit_ref[...],
        (((0,), (0,)), ((), ())),
        preferred_element_type=jnp.float32,
    )


def far_body(column, rows, weight_ref, unit_ref, low_ref, high_ref):
    total = image_sum(weight_ref, unit_ref, pl.ds(column, rows)).astype(jnp.bfloat16)
    low_ref[...] = total[: rows // 2, :]
    high_ref[...] = total[rows // 2 :, :]


def near_body(
    rows, weight_ref, unit_ref, x_high_ref, y_low_ref, x_low_ref, y_high_ref, own_ref
):
    half = rows // 2
    total = image_sum(weight_ref, unit_ref, pl.ds(rows, rows))
    x_low_ref[...] = total[:half, :]
    x_high_ref[...] = total[half:, :].astype(jnp.bfloat16)
    total = image_sum(weight_ref, unit_ref, pl.ds(2 * rows, rows))
    y_low_ref[...] = total[:half, :].astype(jnp.bfloat16)
    y_high_ref[...] = total[half:, :]
    own_ref[...] = image_sum(weight_ref, unit_ref, pl.ds(0, rows))


def relay_body(left_ref, left_in_ref, right_ref, right_in_ref, left_out_ref, right_out_ref):
    left_out_ref[...] = (left_ref[...] + left_in_ref[...].astype(jnp.float32)).astype(jnp.bfloat16)
    right_out_ref[...] = (right_ref[...] + right_in_ref[...].astype(jnp.float32)).astype(
        jnp.bfloat16
    )


def spread_body(rows, weight_ref, unit_ref, out_ref):
    for first in range(0, weight_ref.shape[1], rows):
        out_ref[pl.ds(first, rows), :] = image_sum(
            weight_ref, unit_ref, pl.ds(first, rows)
        ).astype(jnp.bfloat16)


def text_grad_body(tile_count, chunks, raw_ref, acc_ref, add_ref, out_ref):
    width = raw_ref.shape[2]
    for tile in range(tile_count):
        part = pl.ds(tile * TILE, TILE)
        raws = [raw_ref[c, part, :].astype(jnp.float32) for c in range(chunks)]
        scales = row_scales(sum(jnp.sum(x * x, axis=-1, keepdims=True) for x in raws))
        accs = [
            acc_ref[part, pl.ds(c * width, width)]
            + add_ref[part, pl.ds(c * width, width)].astype(jnp.float32)
            for c in range(chunks)
        ]
        units = [x * scales for x in raws]
        inner = sum(jnp.sum(u * a, axis=-1, keepdims=True) for u, a in zip(units, accs))
        for c in range(chunks):
            out_ref[c, part, :] = (scales * (accs[c] - units[c] * inner)).astype(jnp.bfloat16)


def image_grad_body(low_count, high_count, raw_ref, own_ref, *refs):
    low_refs = refs[:low_count]
    high_refs = refs[low_count : low_count + high_count]
    out_ref = refs[-1]
    half = low_refs[0].shape[0]
    step = 64
    for base, adds in ((0, low_refs), (half, high_refs)):
        if not adds:
            continue
        for first in range(0, half, step):
            part = pl.ds(base + first, step)
            raw = raw_ref[part, :].astype(jnp.float32)
            scales = row_scales(jnp.sum(raw * raw, axis=-1, keepdims=True))
            unit = raw * scales
            acc = own_ref[part, :].astype(jnp.float32)
            for ref in adds:
                acc = acc + ref[pl.ds(first, step), :].astype(jnp.float32)
            inner = jnp.sum(unit * acc, axis=-1, keepdims=True)
            out_ref[part, :] = (scales * (acc - unit * inner)).astype(jnp.bfloat16)


def swap(value, count, bit):
    return lax.ppermute(value, "blk", [(b, b ^ bit) for b in range(count)])


def per_device(text_emb, image_emb, logit_scale, logit_bias, bucket, positive, blocks):
    groups = lax.axis_size("tp")
    shards = lax.axis_size("blk")
    rows, embed = image_emb.shape
    tile_count = rows // TILE
    half = rows // 2
    width = text_emb.shape[1]
    chunks = groups
    here = lax.axis_index("blk")
    group = lax.axis_index("tp")
    square = shards == 4 * CORES

    text_own = lax.all_to_all(
        text_emb.reshape(groups, rows, width), "tp", split_axis=0, concat_axis=0, tiled=True
    )
    if square:
        low, high = image_emb[:half], image_emb[half:]
        y_low = swap(low, shards, 4)
        x_high = swap(high, shards, 2)
        x_low = swap(low, shards, 2)
        y_high = swap(high, shards, 4)
        far_low = swap(y_low, shards, 2)
        far_high = swap(x_high, shards, 4)
        pieces = [image_emb, x_low, x_high, y_low, y_high, far_low, far_high]
        sources = [here, here ^ 2, here ^ 4, here ^ 6]
        own_pieces = (0,)
    else:
        same_core = [[chip * CORES + core for chip in range(shards // CORES)] for core in range(CORES)]
        pieces = [
            lax.all_gather(image_emb, "blk", axis=0, tiled=True, axis_index_groups=same_core)
        ]
        sources = [chip * CORES + here % CORES for chip in range(shards // CORES)]
        own_pieces = tuple(range(shards // CORES))
    text_other = swap(text_own, shards, 1)
    piece_rows = [p.shape[0] for p in pieces]
    total_columns = sum(piece_rows)

    def device_rows(vector, shard):
        return lax.dynamic_slice_in_dim(vector, (shard * groups + group) * rows, rows, 0)

    def device_blocks(shard):
        return lax.dynamic_slice_in_dim(
            blocks, (shard * groups + group) * tile_count, tile_count, 0
        )

    text_shards = (here, here ^ 1)
    row_bucket = jnp.concatenate([device_rows(bucket, s) for s in text_shards]).reshape(-1, TILE)
    row_positive = jnp.concatenate([device_rows(positive, s) for s in text_shards]).reshape(
        -1, TILE
    )
    listed = jnp.concatenate([device_blocks(s) for s in text_shards])
    tile_range = jnp.arange(tile_count, dtype=jnp.int32)
    column_buckets = []
    for s in sources:
        entries = lax.dynamic_index_in_dim(listed, s, 1, keepdims=False)
        live = jnp.any(entries[:, None, :] == tile_range[None, :, None], axis=-1)
        tiles = device_rows(bucket, s).reshape(1, tile_count, TILE)
        column_buckets.append(
            jnp.where(live[:, :, None], tiles, -1).reshape(2 * tile_count, rows)
        )
    column_bucket = jnp.concatenate(column_buckets, axis=1)
    column_ids = jnp.concatenate(
        [(s * groups + group) * rows + jnp.arange(rows, dtype=jnp.int32) for s in sources]
    )[None, :]

    pair_flops = 2 * 2 * rows * total_columns * embed
    units, weights, acc_own, acc_other = call_kernel(
        functools.partial(weights_body, tile_count, chunks, piece_rows, own_pieces),
        [
            struct((2 * rows, embed), jnp.bfloat16),
            struct((2 * rows, total_columns), jnp.bfloat16),
            struct((rows, embed), jnp.float32),
            struct((rows, embed), jnp.bfloat16),
        ],
        [logit_scale, logit_bias, text_own, text_other]
        + pieces
        + [row_bucket, row_positive, column_bucket, column_ids],
        [SMEM_SPEC] * 2 + [VMEM_SPEC] * (6 + len(pieces)),
        scratch=[
            pltpu.VMEM((total_columns, embed), jnp.bfloat16),
            pltpu.VMEM((2 * rows, embed), jnp.float32),
        ],
        flops=2 * pair_flops,
        transcendentals=2 * 2 * rows * total_columns,
    )
    acc_in = swap(acc_other, shards, 1)

    def finish_text():
        grad = call_kernel(
            functools.partial(text_grad_body, tile_count, chunks),
            [struct((chunks, rows, width), jnp.bfloat16)],
            [text_own, acc_own, acc_in],
            [VMEM_SPEC] * 3,
        )[0]
        grad = lax.all_to_all(grad, "tp", split_axis=0, concat_axis=0, tiled=True)
        return grad.reshape(groups * rows, width)

    half_bf16 = struct((half, embed), jnp.bfloat16)
    half_f32 = struct((half, embed), jnp.float32)
    full_bf16 = struct((rows, embed), jnp.bfloat16)
    if square:
        to_far_low, to_far_high = call_kernel(
            functools.partial(far_body, 3 * rows, rows),
            [half_bf16, half_bf16],
            [weights, units],
            [VMEM_SPEC] * 2,
            flops=2 * 2 * rows * rows * embed,
        )
        relay_low = swap(to_far_low, shards, 4)
        relay_high = swap(to_far_high, shards, 2)
        text_grad = finish_text()
        to_x_high, to_y_low, near_x_low, near_y_high, own = call_kernel(
            functools.partial(near_body, rows),
            [half_bf16, half_bf16, half_f32, half_f32, struct((rows, embed), jnp.float32)],
            [weights, units],
            [VMEM_SPEC] * 2,
            flops=3 * 2 * 2 * rows * rows * embed,
        )
        from_x_high = swap(to_x_high, shards, 2)
        from_y_low = swap(to_y_low, shards, 4)
        to_x_low, to_y_high = call_kernel(
            relay_body,
            [half_bf16, half_bf16],
            [near_x_low, relay_low, near_y_high, relay_high],
            [VMEM_SPEC] * 4,
        )
        from_x_low = swap(to_x_low, shards, 2)
        from_y_high = swap(to_y_high, shards, 4)
        image_grad = call_kernel(
            functools.partial(image_grad_body, 2, 2),
            [full_bf16],
            [image_emb, own, from_x_low, from_y_low, from_x_high, from_y_high],
            [VMEM_SPEC] * 6,
        )[0]
    else:
        text_grad = finish_text()
        spread = call_kernel(
            functools.partial(spread_body, rows),
            [struct((total_columns, embed), jnp.bfloat16)],
            [weights, units],
            [VMEM_SPEC] * 2,
            flops=pair_flops,
        )[0]
        parts = lax.all_to_all(
            spread, "blk", split_axis=0, concat_axis=0, tiled=True, axis_index_groups=same_core
        )
        total = jnp.sum(
            parts.reshape(-1, rows, embed).astype(jnp.float32), axis=0
        ).reshape(2, half, embed)
        zero = jnp.zeros((half, embed), jnp.bfloat16)
        image_grad = call_kernel(
            functools.partial(image_grad_body, 1, 1),
            [full_bf16],
            [image_emb, total.reshape(rows, embed), zero, zero],
            [VMEM_SPEC] * 4,
        )[0]
    return (text_grad, image_grad)


def solution(mesh):
    in_specs = (P("blk", "tp"), P(("blk", "tp"), None), P(), P(), P(), P(), P())
    out_specs = (P("blk", "tp"), P(("blk", "tp"), None))
    return jax.shard_map(
        per_device, mesh=mesh, in_specs=in_specs, out_specs=out_specs, check_vma=False
    )
```

time: 488 us -> 106 us (0.22)
  other arithmetic: 164 us -> 1.44 us
  local copies, waits for them, and re-layouts: 135 us -> 8.63 us
  matrix products: 107 us -> 0 us
  Pallas kernels: 0 us -> 30.2 us
  between operations: 14.1 us -> 2.12 us
  starting transfers between devices: 11.2 us -> 21.9 us
  waiting for transfers between devices: 51.4 us -> 41.4 us
    dot_general x16 -> x0, matrix products: 107 us -> none  [the longest x8 54.7 us: image_step(): jnp.einsum('cij,cid->cjd', weights, sender_text, preferred_element_type=j...]
    scatter-add x8 -> x0, other arithmetic: 98.4 us -> none  [image_step(): return image_acc.at[local_tile].add(update)]
    gather x57 -> x0, local copies, waits for them, and re-layouts: 47.5 us -> none  [the longest x8 19.1 us: image_step(): mine = image_tiles[local_tile]]
    pallas_call x0 -> x6, Pallas kernels: none -> 30.2 us  [call_kernel(): pl.pallas_call(body, out_shape=outs, in_specs=specs, out_specs=[VMEM_SPEC...]
    reduce_sum x12 -> x0, other arithmetic: 28.9 us -> none  [the longest x8 24.9 us: text_step(): return text_acc + update.reshape(tile_count, SLOTS, TILE, width).sum(axis=1)]
    broadcast_in_dim x34 -> x1, local copies, waits for them, and re-layouts: 28.3 us -> 0.6 us  [per_device(): jnp.concatenate([(s * groups + group) * rows + jnp.arange(rows, dtype=jnp...]
    ppermute x0 -> x14, waiting for transfers between devices: none -> 24.3 us  [swap(): return lax.ppermute(value, 'blk', [(b, b ^ bit) for b in range(count)])]
    all_to_all x2, waiting for transfers between devices: 39.6 us -> 17.1 us  [the longest x1 17.1 us: per_device(): lax.all_to_all(text_emb.reshape(groups, rows, width), 'tp', split_axis=0,...]
  transfers between devices with their start and end apart: 4 -> 16, of which waited for: 3 -> 9; matrix products, arithmetic and copies ran while one was open for 36% -> 4% of each run, Pallas kernels for 0% -> 15%
where the time goes in v1:
time: 106 us
  waiting for transfers between devices  41.4 us (39%)
  Pallas kernels  30.2 us (28%)
  starting transfers between devices  21.9 us (21%)
  local copies, waits for them, and re-layouts  8.63 us (8%)
  between operations  2.12 us (2%)
  other arithmetic  1.44 us (1%)
    pallas_call x6, Pallas kernels, call_kernel(): pl.pallas_call(body, out_shape=outs, in_specs=specs, out_specs=[VMEM_SPEC...  30.2 us
    ppermute x14, waiting for transfers between devices, swap(): return lax.ppermute(value, 'blk', [(b, b ^ bit) for b in range(count)])  24.3 us
    all_to_all x1, waiting for transfers between devices, per_device(): lax.all_to_all(text_emb.reshape(groups, rows, width), 'tp', split_axis=0,...  17.1 us
    ppermute x14, starting transfers between devices, swap(): return lax.ppermute(value, 'blk', [(b, b ^ bit) for b in range(count)])  12.9 us
    all_to_all x1, starting transfers between devices, per_device(): lax.all_to_all(text_emb.reshape(groups, rows, width), 'tp', split_axis=0,...  5.33 us
    unnamed x41, local copies, waits for them, and re-layouts  4.64 us
    all_to_all x1, starting transfers between devices, finish_text(): grad = lax.all_to_all(grad, 'tp', split_axis=0, concat_axis=0, tiled=True)  3.67 us
  transfers between devices with their start and end apart: 16, of which 9 were waited for; matrix products, arithmetic and copies ran while one was open for 4% of the time, Pallas kernels for 15%

profile of v1, /device:TPU:0, one launch (start us, length us, event | category | flops | bytes accessed | tf_op | source)
XLA Modules:
  0.0 105.6 jit_solution(10725886288600761228)
XLA Ops:
  0.6 1.2 %fusion.8 = (bf16[192,1024]{1,0:T(8,128)(2,1)S(1)}, bf16[192,1024]{1,0:T(8,128)(2,1)S(1)}) fusion(bf16[384,1024]{1,0:T(8,128)(2,1)} %raw_ref.1), kind=kLoop, calls=%fused_computation.45 | loop fusion | bytes 1572864 | tf_op jit(solution)/shard_map/slice | solution.py:212
  1.8 3.0 %collective-permute-start.1 = (bf16[192,1024]{1,0:T(8,128)(2,1)S(1)}, bf16[192,1024]{1,0:T(8,128)(2,1)S(1)}, u32[]{:S(2)}, u32[]{:S(2)}) collective-permute-start(bf16[192,1024]{1,0:T(8,128)(2,1)S(1)} %get-tuple-element.29), channel_id=1, source_target_pairs={{0,8},{4,12},{8,0},{12,4},{16,24},{20,28},{24,16},{28,20},{1,9},{5... | collective-permute-start | bytes 1179656 | tf_op jit(solution)/shard_map/ppermute | solution.py:193
  4.8 1.5 %collective-permute-start.3 = (bf16[192,1024]{1,0:T(8,128)(2,1)S(1)}, bf16[192,1024]{1,0:T(8,128)(2,1)S(1)}, u32[]{:S(2)}, u32[]{:S(2)}) collective-permute-start(bf16[192,1024]{1,0:T(8,128)(2,1)S(1)} %get-tuple-element.29), channel_id=1, source_target_pairs={{0,16},{4,20},{8,24},{12,28},{16,0},{20,4},{24,8},{28,12},{1,17},{... | collective-permute-start | bytes 1179656 | tf_op jit(solution)/shard_map/ppermute | solution.py:193
  6.3 0.5 collective-permute-start.2
  6.9 5.3 %all-to-all-start = ((bf16[4,384,256]{2,1,0:T(8,128)(2,1)}), bf16[4,384,256]{2,1,0:T(8,128)(2,1)S(1)}, u32[]{:S(2)}, u32[]{:S(2)}) async-start(bf16[4,384,256]{2,1,0:T(8,128)(2,1)} %bitcast), calls=%async_computation | async-start | bytes 1572864 | tf_op jit(solution)/shard_map/all_to_all | solution.py:208
  12.3 0.1 constant_dynamic-slice_fusion
  12.3 0.1 fusion.5
  12.5 0.1 copy.20
  12.6 0.1 copy.19
  12.7 0.1 copy.18
  12.9 0.1 copy.17
  13.0 0.9 fusion.9
  14.1 0.1 broadcast_bitcast_fusion.3
  14.2 17.1 %all-to-all-done.refs_2_.raw_ref = bf16[4,384,256]{2,1,0:T(8,128)(2,1)S(1)} async-done(((bf16[4,384,256]{2,1,0:T(8,128)(2,1)}), bf16[4,384,256]{2,1,0:T(8,128)(2,1)S(1)}, u32[]{:S(2)}, u32[]{:S(2)}) %all-to-all-start) | async-done | bytes 786464 | tf_op jit(solution)/shard_map/all_to_all | solution.py:208
  31.3 1.6 %collective-permute-start.5 = (bf16[192,1024]{1,0:T(8,128)(2,1)S(1)}, bf16[192,1024]{1,0:T(8,128)(2,1)S(1)}, u32[]{:S(2)}, u32[]{:S(2)}) collective-permute-start(bf16[192,1024]{1,0:T(8,128)(2,1)S(1)} %collective-permute-done.3.refs_7_), channel_id=1, source_target_pairs={{0,8},{4,12},{8,0},{12,4},{16,24},{20,28},{24,16},{28,20},{1,9},{5... | collective-permute-start | bytes 1179656 | tf_op jit(solution)/shard_map/ppermute | solution.py:193
  32.9 1.5 %collective-permute-start.6 = (bf16[192,1024]{1,0:T(8,128)(2,1)S(1)}, bf16[192,1024]{1,0:T(8,128)(2,1)S(1)}, u32[]{:S(2)}, u32[]{:S(2)}) collective-permute-start(bf16[192,1024]{1,0:T(8,128)(2,1)S(1)} %collective-permute-done.2.refs_6_), channel_id=1, source_target_pairs={{0,16},{4,20},{8,24},{12,28},{16,0},{20,4},{24,8},{28,12},{1,17},{... | collective-permute-start | bytes 1179656 | tf_op jit(solution)/shard_map/ppermute | solution.py:193
  34.4 0.8 dynamic-slice_bitcast_fusion.1
  36.5 0.6 broadcast_in_dim.89.refs_14_
  37.1 0.6 pad_add_fusion.2
  37.7 0.6 pad_add_fusion.refs_13_
  38.4 4.5 %collective-permute-done.5.refs_9_ = bf16[192,1024]{1,0:T(8,128)(2,1)S(1)} collective-permute-done((bf16[192,1024]{1,0:T(8,128)(2,1)S(1)}, bf16[192,1024]{1,0:T(8,128)(2,1)S(1)}, u32[]{:S(2)}, u32[]{:S(2)}) %collective-permute-start.5) | collective-permute-done | bytes 393248 | tf_op jit(solution)/shard_map/ppermute | solution.py:193
  42.9 1.2 %collective-permute-done.6.refs_10_ = bf16[192,1024]{1,0:T(8,128)(2,1)S(1)} collective-permute-done((bf16[192,1024]{1,0:T(8,128)(2,1)S(1)}, bf16[192,1024]{1,0:T(8,128)(2,1)S(1)}, u32[]{:S(2)}, u32[]{:S(2)}) %collective-permute-start.6) | collective-permute-done | bytes 393248 | tf_op jit(solution)/shard_map/ppermute | solution.py:193
  44.2 0.8 copy-done.15
  44.9 0.2 copy-done.9
  45.1 11.3 %shard_map.86 = (bf16[768,1024]{1,0:T(8,128)(2,1)}, bf16[768,1536]{1,0:T(8,128)(2,1)}, f32[384,1024]{1,0:T(8,128)}, bf16[384,1024]{1,0:T(8,128)(2,1)}) custom-call(f32[1]{0:T(128)S(6)} %copy.42.refs_0_, f32[1]{0:T(128)S(6)} %copy.43.refs_1_, bf16[4,384,256]{2,1,0:T(8,128)(2,1)} %copy-done, bf16[4,384,256]{2,1,0:T(8,128)(2,1)} %copy-done.9, ...), custom_call_target="tpu_custom_call" | custom-call | flops 4831838208 | bytes 11059208 | tf_op jit(solution)/shard_map/pallas_call | solution.py:25
  56.4 2.5 %collective-permute-done.7.add_ref = bf16[384,1024]{1,0:T(8,128)(2,1)S(1)} collective-permute-done((bf16[384,1024]{1,0:T(8,128)(2,1)}, bf16[384,1024]{1,0:T(8,128)(2,1)S(1)}, u32[]{:S(2)}, u32[]{:S(2)}) %collective-permute-start.7) | collective-permute-done | bytes 786464 | tf_op jit(solution)/shard_map/ppermute | solution.py:193
  58.9 0.9 copy-done.1
  59.8 3.5 %shard_map.87 = bf16[4,384,256]{2,1,0:T(8,128)(2,1)} custom-call(bf16[4,384,256]{2,1,0:T(8,128)(2,1)} %copy-done, f32[384,1024]{1,0:T(8,128)} %get-tuple-element.15.acc_ref, bf16[384,1024]{1,0:T(8,128)(2,1)} %copy-done.1), custom_call_target="tpu_custom_call" | custom-call | bytes 3932160 | tf_op jit(solution)/shard_map/pallas_call | solution.py:25
  63.3 3.7 %all-to-all-start.1 = ((bf16[4,384,256]{2,1,0:T(8,128)(2,1)}), bf16[4,384,256]{2,1,0:T(8,128)(2,1)S(1)}, u32[]{:S(2)}, u32[]{:S(2)}) async-start(bf16[4,384,256]{2,1,0:T(8,128)(2,1)} %shard_map.87), calls=%async_computation.1 | async-start | bytes 1572864 | tf_op jit(solution)/shard_map/all_to_all | solution.py:290
  67.0 3.8 %shard_map.89 = (bf16[192,1024]{1,0:T(8,128)(2,1)}, bf16[192,1024]{1,0:T(8,128)(2,1)}) custom-call(bf16[768,1536]{1,0:T(8,128)(2,1)} %get-tuple-element.17.weight_ref, bf16[768,1024]{1,0:T(8,128)(2,1)} %get-tuple-element.18.unit_ref), custom_call_target="tpu_custom_call" | custom-call | flops 603979776 | bytes 4718592 | tf_op jit(solution)/shard_map/pallas_call | solution.py:25
  70.7 1.5 %collective-permute-start.8 = (bf16[192,1024]{1,0:T(8,128)(2,1)}, bf16[192,1024]{1,0:T(8,128)(2,1)S(1)}, u32[]{:S(2)}, u32[]{:S(2)}) collective-permute-start(bf16[192,1024]{1,0:T(8,128)(2,1)} %get-tuple-element.21), channel_id=1, source_target_pairs={{0,16},{4,20},{8,24},{12,28},{16,0},{20,4},{24,8},{28,12},{1,17},{... | collective-permute-start | bytes 1179656 | tf_op jit(solution)/shard_map/ppermute | solution.py:193
  72.3 0.5 collective-permute-start.9
  72.8 5.3 %shard_map.88 = (bf16[192,1024]{1,0:T(8,128)(2,1)}, bf16[192,1024]{1,0:T(8,128)(2,1)}, f32[192,1024]{1,0:T(8,128)}, f32[192,1024]{1,0:T(8,128)}, f32[384,1024]{1,0:T(8,128)}) custom-call(bf16[768,1536]{1,0:T(8,128)(2,1)} %get-tuple-element.17.weight_ref, bf16[768,1024]{1,0:T(8,128)(2,1)} %get-tuple-element.18.unit_ref), custom_call_target="tpu_custom_call" | custom-call | flops 1811939328 | bytes 7864320 | tf_op jit(solution)/shard_map/pallas_call | solution.py:25
  78.1 0.5 collective-permute-start.11
  78.6 1.5 %collective-permute-start.12 = (bf16[192,1024]{1,0:T(8,128)(2,1)}, bf16[192,1024]{1,0:T(8,128)(2,1)S(1)}, u32[]{:S(2)}, u32[]{:S(2)}) collective-permute-start(bf16[192,1024]{1,0:T(8,128)(2,1)} %get-tuple-element.26), channel_id=1, source_target_pairs={{0,8},{4,12},{8,0},{12,4},{16,24},{20,28},{24,16},{28,20},{1,9},{5... | collective-permute-start | bytes 1179656 | tf_op jit(solution)/shard_map/ppermute | solution.py:193
  80.1 2.8 %collective-permute-done.8.left_in_ref = bf16[192,1024]{1,0:T(8,128)(2,1)S(1)} collective-permute-done((bf16[192,1024]{1,0:T(8,128)(2,1)}, bf16[192,1024]{1,0:T(8,128)(2,1)S(1)}, u32[]{:S(2)}, u32[]{:S(2)}) %collective-permute-start.8) | collective-permute-done | bytes 393248 | tf_op jit(solution)/shard_map/ppermute | solution.py:193
  82.9 1.6 %collective-permute-done.9.right_in_ref = bf16[192,1024]{1,0:T(8,128)(2,1)S(1)} collective-permute-done((bf16[192,1024]{1,0:T(8,128)(2,1)}, bf16[192,1024]{1,0:T(8,128)(2,1)S(1)}, u32[]{:S(2)}, u32[]{:S(2)}) %collective-permute-start.9) | collective-permute-done | bytes 393248 | tf_op jit(solution)/shard_map/ppermute | solution.py:193
  84.5 0.7 copy-done.5
  85.2 2.6 %shard_map.90 = (bf16[192,1024]{1,0:T(8,128)(2,1)}, bf16[192,1024]{1,0:T(8,128)(2,1)}) custom-call(f32[192,1024]{1,0:T(8,128)} %get-tuple-element.20.left_ref, bf16[192,1024]{1,0:T(8,128)(2,1)} %copy-done.4, f32[192,1024]{1,0:T(8,128)} %get-tuple-element.22.right_ref, bf16[192,1024]{1,0:T(8,128)(2,1)} %copy-done.5), custom_call_target="tpu_custom_call" | custom-call | bytes 3145728 | tf_op jit(solution)/shard_map/pallas_call | solution.py:25
  87.8 0.5 collective-permute-start.10
  88.4 0.1 collective-permute-start.13
  88.5 2.9 %collective-permute-done.11.refs_1_ = bf16[192,1024]{1,0:T(8,128)(2,1)S(1)} collective-permute-done((bf16[192,1024]{1,0:T(8,128)(2,1)}, bf16[192,1024]{1,0:T(8,128)(2,1)S(1)}, u32[]{:S(2)}, u32[]{:S(2)}) %collective-permute-start.11) | collective-permute-done | bytes 393248 | tf_op jit(solution)/shard_map/ppermute | solution.py:193
  91.3 1.6 %collective-permute-done.12.refs_2_ = bf16[192,1024]{1,0:T(8,128)(2,1)S(1)} collective-permute-done((bf16[192,1024]{1,0:T(8,128)(2,1)}, bf16[192,1024]{1,0:T(8,128)(2,1)S(1)}, u32[]{:S(2)}, u32[]{:S(2)}) %collective-permute-start.12) | collective-permute-done | bytes 393248 | tf_op jit(solution)/shard_map/ppermute | solution.py:193
  92.9 7.3 %collective-permute-done.10.refs_0_ = bf16[192,1024]{1,0:T(8,128)(2,1)S(1)} collective-permute-done((bf16[192,1024]{1,0:T(8,128)(2,1)}, bf16[192,1024]{1,0:T(8,128)(2,1)S(1)}, u32[]{:S(2)}, u32[]{:S(2)}) %collective-permute-start.10) | collective-permute-done | bytes 393248 | tf_op jit(solution)/shard_map/ppermute | solution.py:193
  100.2 0.7 copy-done.6
  101.0 0.1 copy-done.7
  101.1 3.6 %shard_map.91 = bf16[384,1024]{1,0:T(8,128)(2,1)} custom-call(bf16[384,1024]{1,0:T(8,128)(2,1)} %raw_ref.1, f32[384,1024]{1,0:T(8,128)} %get-tuple-element.19.own_ref, bf16[192,1024]{1,0:T(8,128)(2,1)} %copy-done.6, bf16[192,1024]{1,0:T(8,128)(2,1)} %copy-done.2, bf16[192,1024]{1,0:T(8,128)(2,1)} %copy-done.3, bf16[192,1024]{1,0:T(8,128)(2,1)} %copy-done.7), custom_call_target="tpu_custom_call" | custom-call | bytes 4718592 | tf_op jit(solution)/shard_map/pallas_call | solution.py:25
  104.7 0.9 copy.44
  (52 shorter events, 0.5 us)
Async XLA Ops:
  0.6 11.6 %copy-start.8 = (s32[96,8,3]{0,1,2:T(8,128)S(1)}, s32[96,8,3]{0,1,2:T(8,128)}, u32[]{:S(2)}) copy-start(s32[96,8,3]{0,1,2:T(8,128)} %param.13) | copy-start | bytes 27652
  1.8 36.5 %collective-permute-start.1 = (bf16[192,1024]{1,0:T(8,128)(2,1)S(1)}, bf16[192,1024]{1,0:T(8,128)(2,1)S(1)}, u32[]{:S(2)}, u32[]{:S(2)}) collective-permute-start(bf16[192,1024]{1,0:T(8,128)(2,1)S(1)} %get-tuple-element.29), channel_id=1, source_target_pairs={{0,8},{4,12},{8,0},{12,4},{16,24},{20,28},{24,16},{28,20},{1,9},{5... | collective-permute-start | bytes 1179656 | tf_op jit(solution)/shard_map/ppermute | solution.py:193
  4.8 26.5 %collective-permute-start.3 = (bf16[192,1024]{1,0:T(8,128)(2,1)S(1)}, bf16[192,1024]{1,0:T(8,128)(2,1)S(1)}, u32[]{:S(2)}, u32[]{:S(2)}) collective-permute-start(bf16[192,1024]{1,0:T(8,128)(2,1)S(1)} %get-tuple-element.29), channel_id=1, source_target_pairs={{0,16},{4,20},{8,24},{12,28},{16,0},{20,4},{24,8},{28,12},{1,17},{... | collective-permute-start | bytes 1179656 | tf_op jit(solution)/shard_map/ppermute | solution.py:193
  6.3 26.5 %collective-permute-start.2 = (bf16[192,1024]{1,0:T(8,128)(2,1)S(1)}, bf16[192,1024]{1,0:T(8,128)(2,1)S(1)}, u32[]{:S(2)}, u32[]{:S(2)}) collective-permute-start(bf16[192,1024]{1,0:T(8,128)(2,1)S(1)} %get-tuple-element.28), channel_id=1, source_target_pairs={{0,8},{4,12},{8,0},{12,4},{16,24},{20,28},{24,16},{28,20},{1,9},{5... | collective-permute-start | bytes 1179656 | tf_op jit(solution)/shard_map/ppermute | solution.py:193
  6.9 31.5 %collective-permute-start.4 = (bf16[192,1024]{1,0:T(8,128)(2,1)S(1)}, bf16[192,1024]{1,0:T(8,128)(2,1)S(1)}, u32[]{:S(2)}, u32[]{:S(2)}) collective-permute-start(bf16[192,1024]{1,0:T(8,128)(2,1)S(1)} %get-tuple-element.28), channel_id=1, source_target_pairs={{0,16},{4,20},{8,24},{12,28},{16,0},{20,4},{24,8},{28,12},{1,17},{... | collective-permute-start | bytes 1179656 | tf_op jit(solution)/shard_map/ppermute | solution.py:193
  6.9 24.3 %all-to-all-start = ((bf16[4,384,256]{2,1,0:T(8,128)(2,1)}), bf16[4,384,256]{2,1,0:T(8,128)(2,1)S(1)}, u32[]{:S(2)}, u32[]{:S(2)}) async-start(bf16[4,384,256]{2,1,0:T(8,128)(2,1)} %bitcast), calls=%async_computation | async-start | bytes 1572864 | tf_op jit(solution)/shard_map/all_to_all | solution.py:208
  31.2 12.9 %copy-start = (bf16[4,384,256]{2,1,0:T(8,128)(2,1)}, bf16[4,384,256]{2,1,0:T(8,128)(2,1)S(1)}, u32[]{:S(2)}) copy-start(bf16[4,384,256]{2,1,0:T(8,128)(2,1)S(1)} %all-to-all-done.refs_2_.raw_ref) | copy-start | bytes 2359300
  31.2 12.9 %collective-permute-start = (bf16[4,384,256]{2,1,0:T(8,128)(2,1)S(1)}, bf16[4,384,256]{2,1,0:T(8,128)(2,1)S(1)}, u32[]{:S(2)}, u32[]{:S(2)}) collective-permute-start(bf16[4,384,256]{2,1,0:T(8,128)(2,1)S(1)} %all-to-all-done.refs_2_.raw_ref), channel_id=1, source_target_pairs={{0,4},{4,0},{8,12},{12,8},{16,20},{20,16},{24,28},{28,24},{1,5},{5... | collective-permute-start | bytes 2359304 | tf_op jit(solution)/shard_map/ppermute | solution.py:193
  31.3 12.8 %copy-start.11 = (bf16[192,1024]{1,0:T(8,128)(2,1)}, bf16[192,1024]{1,0:T(8,128)(2,1)S(1)}, u32[]{:S(2)}) copy-start(bf16[192,1024]{1,0:T(8,128)(2,1)S(1)} %collective-permute-done.3.refs_7_) | copy-start | bytes 1179652
  31.3 11.6 %collective-permute-start.5 = (bf16[192,1024]{1,0:T(8,128)(2,1)S(1)}, bf16[192,1024]{1,0:T(8,128)(2,1)S(1)}, u32[]{:S(2)}, u32[]{:S(2)}) collective-permute-start(bf16[192,1024]{1,0:T(8,128)(2,1)S(1)} %collective-permute-done.3.refs_7_), channel_id=1, source_target_pairs={{0,8},{4,12},{8,0},{12,4},{16,24},{20,28},{24,16},{28,20},{1,9},{5... | collective-permute-start | bytes 1179656 | tf_op jit(solution)/shard_map/ppermute | solution.py:193
  32.9 11.3 %copy-start.12 = (bf16[192,1024]{1,0:T(8,128)(2,1)}, bf16[192,1024]{1,0:T(8,128)(2,1)S(1)}, u32[]{:S(2)}) copy-start(bf16[192,1024]{1,0:T(8,128)(2,1)S(1)} %collective-permute-done.2.refs_6_) | copy-start | bytes 1179652
  32.9 11.2 %collective-permute-start.6 = (bf16[192,1024]{1,0:T(8,128)(2,1)S(1)}, bf16[192,1024]{1,0:T(8,128)(2,1)S(1)}, u32[]{:S(2)}, u32[]{:S(2)}) collective-permute-start(bf16[192,1024]{1,0:T(8,128)(2,1)S(1)} %collective-permute-done.2.refs_6_), channel_id=1, source_target_pairs={{0,16},{4,20},{8,24},{12,28},{16,0},{20,4},{24,8},{28,12},{1,17},{... | collective-permute-start | bytes 1179656 | tf_op jit(solution)/shard_map/ppermute | solution.py:193
  38.3 5.8 %copy-start.10 = (bf16[192,1024]{1,0:T(8,128)(2,1)}, bf16[192,1024]{1,0:T(8,128)(2,1)S(1)}, u32[]{:S(2)}) copy-start(bf16[192,1024]{1,0:T(8,128)(2,1)S(1)} %collective-permute-done.1.refs_5_) | copy-start | bytes 1179652
  38.4 5.8 %copy-start.13 = (bf16[192,1024]{1,0:T(8,128)(2,1)}, bf16[192,1024]{1,0:T(8,128)(2,1)S(1)}, u32[]{:S(2)}) copy-start(bf16[192,1024]{1,0:T(8,128)(2,1)S(1)} %collective-permute-done.4.refs_8_) | copy-start | bytes 1179652
  42.9 1.3 %copy-start.14 = (bf16[192,1024]{1,0:T(8,128)(2,1)}, bf16[192,1024]{1,0:T(8,128)(2,1)S(1)}, u32[]{:S(2)}) copy-start(bf16[192,1024]{1,0:T(8,128)(2,1)S(1)} %collective-permute-done.5.refs_9_) | copy-start | bytes 1179652
  44.1 0.8 copy-start.15
  44.1 1.0 copy-start.9
  56.4 2.5 %collective-permute-start.7 = (bf16[384,1024]{1,0:T(8,128)(2,1)}, bf16[384,1024]{1,0:T(8,128)(2,1)S(1)}, u32[]{:S(2)}, u32[]{:S(2)}) collective-permute-start(bf16[384,1024]{1,0:T(8,128)(2,1)} %get-tuple-element.16), channel_id=1, source_target_pairs={{0,4},{4,0},{8,12},{12,8},{16,20},{20,16},{24,28},{28,24},{1,5},{5... | collective-permute-start | bytes 2359304 | tf_op jit(solution)/shard_map/ppermute | solution.py:193
  58.9 0.9 copy-start.1
  63.3 41.4 %all-to-all-start.1 = ((bf16[4,384,256]{2,1,0:T(8,128)(2,1)}), bf16[4,384,256]{2,1,0:T(8,128)(2,1)S(1)}, u32[]{:S(2)}, u32[]{:S(2)}) async-start(bf16[4,384,256]{2,1,0:T(8,128)(2,1)} %shard_map.87), calls=%async_computation.1 | async-start | bytes 1572864 | tf_op jit(solution)/shard_map/all_to_all | solution.py:290
  70.7 12.2 %collective-permute-start.8 = (bf16[192,1024]{1,0:T(8,128)(2,1)}, bf16[192,1024]{1,0:T(8,128)(2,1)S(1)}, u32[]{:S(2)}, u32[]{:S(2)}) collective-permute-start(bf16[192,1024]{1,0:T(8,128)(2,1)} %get-tuple-element.21), channel_id=1, source_target_pairs={{0,16},{4,20},{8,24},{12,28},{16,0},{20,4},{24,8},{28,12},{1,17},{... | collective-permute-start | bytes 1179656 | tf_op jit(solution)/shard_map/ppermute | solution.py:193
  72.3 12.2 %collective-permute-start.9 = (bf16[192,1024]{1,0:T(8,128)(2,1)}, bf16[192,1024]{1,0:T(8,128)(2,1)S(1)}, u32[]{:S(2)}, u32[]{:S(2)}) collective-permute-start(bf16[192,1024]{1,0:T(8,128)(2,1)} %get-tuple-element.23), channel_id=1, source_target_pairs={{0,8},{4,12},{8,0},{12,4},{16,24},{20,28},{24,16},{28,20},{1,9},{5... | collective-permute-start | bytes 1179656 | tf_op jit(solution)/shard_map/ppermute | solution.py:193
  78.1 13.2 %collective-permute-start.11 = (bf16[192,1024]{1,0:T(8,128)(2,1)}, bf16[192,1024]{1,0:T(8,128)(2,1)S(1)}, u32[]{:S(2)}, u32[]{:S(2)}) collective-permute-start(bf16[192,1024]{1,0:T(8,128)(2,1)} %get-tuple-element.25), channel_id=1, source_target_pairs={{0,16},{4,20},{8,24},{12,28},{16,0},{20,4},{24,8},{28,12},{1,17},{... | collective-permute-start | bytes 1179656 | tf_op jit(solution)/shard_map/ppermute | solution.py:193
  78.6 14.3 %collective-permute-start.12 = (bf16[192,1024]{1,0:T(8,128)(2,1)}, bf16[192,1024]{1,0:T(8,128)(2,1)S(1)}, u32[]{:S(2)}, u32[]{:S(2)}) collective-permute-start(bf16[192,1024]{1,0:T(8,128)(2,1)} %get-tuple-element.26), channel_id=1, source_target_pairs={{0,8},{4,12},{8,0},{12,4},{16,24},{20,28},{24,16},{28,20},{1,9},{5... | collective-permute-start | bytes 1179656 | tf_op jit(solution)/shard_map/ppermute | solution.py:193
  82.9 1.6 %copy-start.4 = (bf16[192,1024]{1,0:T(8,128)(2,1)}, bf16[192,1024]{1,0:T(8,128)(2,1)S(1)}, u32[]{:S(2)}) copy-start(bf16[192,1024]{1,0:T(8,128)(2,1)S(1)} %collective-permute-done.8.left_in_ref) | copy-start | bytes 1179652
  84.5 0.7 copy-start.5
  87.8 12.4 %collective-permute-start.10 = (bf16[192,1024]{1,0:T(8,128)(2,1)}, bf16[192,1024]{1,0:T(8,128)(2,1)S(1)}, u32[]{:S(2)}, u32[]{:S(2)}) collective-permute-start(bf16[192,1024]{1,0:T(8,128)(2,1)} %get-tuple-element.24), channel_id=1, source_target_pairs={{0,8},{4,12},{8,0},{12,4},{16,24},{20,28},{24,16},{28,20},{1,9},{5... | collective-permute-start | bytes 1179656 | tf_op jit(solution)/shard_map/ppermute | solution.py:193
  88.4 11.9 %collective-permute-start.13 = (bf16[192,1024]{1,0:T(8,128)(2,1)}, bf16[192,1024]{1,0:T(8,128)(2,1)S(1)}, u32[]{:S(2)}, u32[]{:S(2)}) collective-permute-start(bf16[192,1024]{1,0:T(8,128)(2,1)} %get-tuple-element.27), channel_id=1, source_target_pairs={{0,16},{4,20},{8,24},{12,28},{16,0},{20,4},{24,8},{28,12},{1,17},{... | collective-permute-start | bytes 1179656 | tf_op jit(solution)/shard_map/ppermute | solution.py:193
  91.3 8.9 %copy-start.2 = (bf16[192,1024]{1,0:T(8,128)(2,1)}, bf16[192,1024]{1,0:T(8,128)(2,1)S(1)}, u32[]{:S(2)}) copy-start(bf16[192,1024]{1,0:T(8,128)(2,1)S(1)} %collective-permute-done.11.refs_1_) | copy-start | bytes 1179652
  92.9 7.3 %copy-start.3 = (bf16[192,1024]{1,0:T(8,128)(2,1)}, bf16[192,1024]{1,0:T(8,128)(2,1)S(1)}, u32[]{:S(2)}) copy-start(bf16[192,1024]{1,0:T(8,128)(2,1)S(1)} %collective-permute-done.12.refs_2_) | copy-start | bytes 1179652
  100.2 0.7 copy-start.6
  100.2 0.9 copy-start.7

commit v2 on v0

v2 whole, which is shorter than its diff:
```python
import functools
import math

import jax
import jax.numpy as jnp
from jax import lax
from jax.experimental import pallas as pl
from jax.experimental.pallas import tpu as pltpu
from jax.sharding import PartitionSpec as P

TILE = 128
SLOTS = 3
CORES = 2
EPS = 1e-06
LOG2E = math.log2(math.e)
MIB = 1024 * 1024

VMEM_SPEC = pl.BlockSpec(memory_space=pltpu.VMEM)
SMEM_SPEC = pl.BlockSpec(memory_space=pltpu.SMEM)


def call_kernel(body, outs, operands, scalars=0, scratch=(), flops=0, transcendentals=0, limit=24):
    moved = sum(x.size * x.dtype.itemsize for x in operands)
    moved += sum(math.prod(o.shape) * o.dtype.itemsize for o in outs)
    return pl.pallas_call(
        body,
        out_shape=outs,
        in_specs=[SMEM_SPEC] * scalars + [VMEM_SPEC] * (len(operands) - scalars),
        out_specs=[VMEM_SPEC] * len(outs),
        scratch_shapes=list(scratch),
        compiler_params=pltpu.CompilerParams(vmem_limit_bytes=limit * MIB),
        cost_estimate=pl.CostEstimate(
            flops=flops, bytes_accessed=moved, transcendentals=transcendentals
        ),
    )(*operands)


def struct(shape, dtype):
    return jax.ShapeDtypeStruct(shape, dtype)


def row_scales(square_sum):
    return lax.rsqrt(square_sum + EPS)


def column_of(row):
    return jnp.broadcast_to(row, (TILE, TILE)).T


def dot_nt(left, right):
    return lax.dot_general(
        left, right, (((1,), (1,)), ((), ())), preferred_element_type=jnp.float32
    )


def dot_tn(left, right):
    return lax.dot_general(
        left, right, (((0,), (0,)), ((), ())), preferred_element_type=jnp.float32
    )


def feature_slice(place, k, width):
    return pl.ds(pl.multiple_of((place ^ k) * width, width), width)


def unit_text(place, chunk_refs, unit_ref, base):
    rows, width = chunk_refs[0].shape
    for first in range(0, rows, TILE):
        part = pl.ds(first, TILE)
        parts = [ref[part, :].astype(jnp.float32) for ref in chunk_refs]
        scales = row_scales(sum(jnp.sum(x * x, axis=-1, keepdims=True) for x in parts))
        for k, x in enumerate(parts):
            unit_ref[pl.ds(base + first, TILE), feature_slice(place, k, width)] = (
                x * scales
            ).astype(jnp.bfloat16)


def unit_images(piece_refs, image_ref):
    start = 0
    step = 64
    for ref in piece_refs:
        for first in range(0, ref.shape[0], step):
            values = ref[pl.ds(first, step), :].astype(jnp.float32)
            scales = row_scales(jnp.sum(values * values, axis=-1, keepdims=True))
            image_ref[pl.ds(start + first, step), :] = (values * scales).astype(jnp.bfloat16)
        start += ref.shape[0]


def pair_weights(scale, bias, products, meta_refs, column, own_rows, weight_ref):
    rowb_ref, pos_ref, colb_ref, colid_ref = meta_refs
    slope = -scale * LOG2E
    offset = -bias * LOG2E
    rows, columns = products.shape
    for a in range(rows // TILE):
        row_bucket = column_of(rowb_ref[pl.ds(a, 1), :])
        own = a * TILE < own_rows
        row_positive = column_of(pos_ref[pl.ds(a, 1), :]) if own else None
        for j in range(columns // TILE):
            lanes = pl.ds(column + j * TILE, TILE)
            power = (
                products[a * TILE : (a + 1) * TILE, j * TILE : (j + 1) * TILE] * slope + offset
            )
            factor = jnp.where(row_bucket == colb_ref[pl.ds(a, 1), lanes], scale, 0.0)
            if own:
                matched = row_positive == colid_ref[:, lanes]
                power = jnp.where(matched, -power, power)
                factor = jnp.where(matched, -scale, factor)
            below = 1.0 + jnp.exp2(power)
            inverse = pl.reciprocal(below, approx=True)
            inverse = inverse * (2.0 - below * inverse)
            weight_ref[pl.ds(a * TILE, TILE), lanes] = (factor * inverse).astype(jnp.bfloat16)


def near_body(chunks, *refs):
    scale_ref, bias_ref, place_ref = refs[:3]
    own_chunks, other_chunks = refs[3 : 3 + chunks], refs[3 + chunks : 3 + 2 * chunks]
    refs = refs[3 + 2 * chunks :]
    piece_refs, meta_refs = refs[:3], refs[3:7]
    x_high_ref, y_low_ref, x_low_ref, y_high_ref, unit_ref, acc_ref, own_weight_ref = refs[7:14]
    image_ref, weight_ref = refs[14:]
    rows = piece_refs[0].shape[0]
    half = rows // 2
    place = place_ref[0]
    scale, bias = scale_ref[0], bias_ref[0]
    unit_text(place, own_chunks, unit_ref, 0)
    unit_text(place, other_chunks, unit_ref, rows)
    unit_images(piece_refs, image_ref)
    order = (1, 2, 0)
    group = [pl.ds(q * rows, rows) for q in range(3)]
    products = dot_nt(unit_ref[...], image_ref[group[order[0]], :])
    for at, q in enumerate(order):
        now = products
        if at + 1 < len(order):
            products = dot_nt(unit_ref[...], image_ref[group[order[at + 1]], :])
        pair_weights(scale, bias, now, meta_refs, q * rows, rows if q == 0 else 0, weight_ref)
        if q == 0:
            own_weight_ref[...] = weight_ref[:, group[0]]
            continue
        total = dot_tn(weight_ref[:, group[q]], unit_ref[...])
        if q == 1:
            x_low_ref[...] = total[:half, :]
            x_high_ref[...] = total[half:, :].astype(jnp.bfloat16)
        else:
            y_low_ref[...] = total[:half, :].astype(jnp.bfloat16)
            y_high_ref[...] = total[half:, :]
    acc_ref[...] = jnp.dot(weight_ref[...], image_ref[...], preferred_element_type=jnp.float32)


def far_body(*refs):
    scale_ref, bias_ref = refs[:2]
    unit_ref, acc_ref = refs[2:4]
    piece_refs, meta_refs = refs[4:6], refs[6:10]
    low_ref, high_ref, acc_own_ref, acc_other_ref, image_ref, weight_ref = refs[10:]
    half = piece_refs[0].shape[0]
    rows = 2 * half
    unit_images(piece_refs, image_ref)
    products = dot_nt(unit_ref[...], image_ref[...])
    pair_weights(scale_ref[0], bias_ref[0], products, meta_refs, 0, 0, weight_ref)
    update = jnp.dot(weight_ref[...], image_ref[...], preferred_element_type=jnp.float32)
    acc_other_ref[...] = (acc_ref[rows:, :] + update[rows:, :]).astype(jnp.bfloat16)
    acc_own_ref[...] = acc_ref[:rows, :] + update[:rows, :]
    total = dot_tn(weight_ref[...], unit_ref[...]).astype(jnp.bfloat16)
    low_ref[...] = total[:half, :]
    high_ref[...] = total[half:, :]


def own_body(weight_ref, unit_ref, out_ref):
    out_ref[...] = dot_tn(weight_ref[...], unit_ref[...])


def all_body(chunks, *refs):
    scale_ref, bias_ref, place_ref = refs[:3]
    own_chunks, other_chunks = refs[3 : 3 + chunks], refs[3 + chunks : 3 + 2 * chunks]
    refs = refs[3 + 2 * chunks :]
    piece_ref, meta_refs = refs[0], refs[1:5]
    spread_ref, acc_own_ref, acc_other_ref, unit_ref, image_ref, weight_ref, acc_ref = refs[5:]
    rows = own_chunks[0].shape[0]
    place = place_ref[0]
    unit_text(place, own_chunks, unit_ref, 0)
    unit_text(place, other_chunks, unit_ref, rows)
    unit_images([piece_ref], image_ref)
    for first in range(0, piece_ref.shape[0], rows):
        group = pl.ds(first, rows)
        products = dot_nt(unit_ref[...], image_ref[group, :])
        pair_weights(scale_ref[0], bias_ref[0], products, meta_refs, first, rows, weight_ref)
        weights = weight_ref[:, group]
        update = jnp.dot(weights, image_ref[group, :], preferred_element_type=jnp.float32)
        acc_ref[...] = update if first == 0 else acc_ref[...] + update
        spread_ref[group, :] = dot_tn(weights, unit_ref[...]).astype(jnp.bfloat16)
    acc_own_ref[...] = acc_ref[:rows, :]
    acc_other_ref[...] = acc_ref[rows:, :].astype(jnp.bfloat16)


def relay_body(left_ref, left_in_ref, right_ref, right_in_ref, left_out_ref, right_out_ref):
    left_out_ref[...] = (left_ref[...] + left_in_ref[...].astype(jnp.float32)).astype(jnp.bfloat16)
    right_out_ref[...] = (right_ref[...] + right_in_ref[...].astype(jnp.float32)).astype(
        jnp.bfloat16
    )


def text_grad_body(chunks, *refs):
    place_ref = refs[0]
    raw_refs = refs[1 : 1 + chunks]
    acc_ref, add_ref = refs[1 + chunks : 3 + chunks]
    out_refs = refs[3 + chunks :]
    place = place_ref[0]
    rows, width = raw_refs[0].shape
    for first in range(0, rows, TILE):
        part = pl.ds(first, TILE)
        raws = [ref[part, :].astype(jnp.float32) for ref in raw_refs]
        scales = row_scales(sum(jnp.sum(x * x, axis=-1, keepdims=True) for x in raws))
        accs = []
        for k in range(chunks):
            features = feature_slice(place, k, width)
            accs.append(acc_ref[part, features] + add_ref[part, features].astype(jnp.float32))
        units = [x * scales for x in raws]
        inner = sum(jnp.sum(u * a, axis=-1, keepdims=True) for u, a in zip(units, accs))
        for k in range(chunks):
            out_refs[k][part, :] = (scales * (accs[k] - units[k] * inner)).astype(jnp.bfloat16)


def finish_body(chunks, low_count, high_count, *refs):
    place_ref = refs[0]
    text_refs = refs[1 : 1 + chunks]
    raw_ref, own_ref = refs[1 + chunks : 3 + chunks]
    refs = refs[3 + chunks :]
    low_refs, high_refs = refs[:low_count], refs[low_count : low_count + high_count]
    text_out_ref, image_out_ref = refs[low_count + high_count :]
    place = place_ref[0]
    rows = raw_ref.shape[0]
    half = rows // 2
    step = 64
    for base, adds in ((0, low_refs), (half, high_refs)):
        for first in range(0, half, step):
            part = pl.ds(base + first, step)
            raw = raw_ref[part, :].astype(jnp.float32)
            scales = row_scales(jnp.sum(raw * raw, axis=-1, keepdims=True))
            unit = raw * scales
            acc = own_ref[part, :].astype(jnp.float32)
            for ref in adds:
                acc = acc + ref[pl.ds(first, step), :].astype(jnp.float32)
            inner = jnp.sum(unit * acc, axis=-1, keepdims=True)
            image_out_ref[part, :] = (scales * (acc - unit * inner)).astype(jnp.bfloat16)
    for k in range(chunks):
        text_out_ref[pl.ds(pl.multiple_of((place ^ k) * rows, rows), rows), :] = text_refs[k][...]


def swap(value, axis, bits):
    count = lax.axis_size(axis)
    return lax.ppermute(value, axis, [(i, i ^ bits) for i in range(count)])


def per_device(text_emb, image_emb, logit_scale, logit_bias, bucket, positive, blocks):
    groups = lax.axis_size("tp")
    shards = lax.axis_size("blk")
    rows, embed = image_emb.shape
    tile_count = rows // TILE
    half = rows // 2
    width = text_emb.shape[1]
    here = lax.axis_index("blk")
    group = lax.axis_index("tp")
    place = group.astype(jnp.int32).reshape(1)
    square = shards == 4 * CORES
    same_core = [[chip * CORES + core for chip in range(shards // CORES)] for core in range(CORES)]

    def text_rows(k):
        return lax.dynamic_slice_in_dim(text_emb, (group ^ k) * rows, rows, 0)

    if square:
        from_x = swap(image_emb, "blk", 2)
        from_y = swap(image_emb, "blk", 4)
        sources = [here, here ^ 2, here ^ 4, here ^ 6]
    else:
        gathered = lax.all_gather(
            image_emb, "blk", axis=0, tiled=True, axis_index_groups=same_core
        )
        sources = [chip * CORES + here % CORES for chip in range(shards // CORES)]
    text_own = [text_rows(0)] + [swap(text_rows(k), "tp", k) for k in range(1, groups)]
    text_other = [swap(chunk, "blk", 1) for chunk in text_own]

    def device_rows(vector, shard):
        return lax.dynamic_slice_in_dim(vector, (shard * groups + group) * rows, rows, 0)

    def device_blocks(shard):
        return lax.dynamic_slice_in_dim(
            blocks, (shard * groups + group) * tile_count, tile_count, 0
        )

    text_shards = (here, here ^ 1)
    row_bucket = jnp.concatenate([device_rows(bucket, s) for s in text_shards]).reshape(-1, TILE)
    row_positive = jnp.concatenate([device_rows(positive, s) for s in text_shards]).reshape(
        -1, TILE
    )
    listed = jnp.concatenate([device_blocks(s) for s in text_shards])
    tile_range = jnp.arange(tile_count, dtype=jnp.int32)

    def meta(shard_list):
        buckets = []
        for s in shard_list:
            entries = lax.dynamic_index_in_dim(listed, s, 1, keepdims=False)
            live = jnp.any(entries[:, None, :] == tile_range[None, :, None], axis=-1)
            tiles = device_rows(bucket, s).reshape(1, tile_count, TILE)
            buckets.append(jnp.where(live[:, :, None], tiles, -1).reshape(2 * tile_count, rows))
        ids = [
            (s * groups + group) * rows + jnp.arange(rows, dtype=jnp.int32) for s in shard_list
        ]
        return [
            row_bucket,
            row_positive,
            jnp.concatenate(buckets, axis=1),
            jnp.concatenate(ids)[None, :],
        ]

    def bf16(count, columns=embed):
        return struct((count, columns), jnp.bfloat16)

    def f32(count, columns=embed):
        return struct((count, columns), jnp.float32)

    both = 2 * rows
    unit_flops = 2 * both * rows * embed
    scalars = [logit_scale, logit_bias]

    def finish_text(acc_own, acc_other):
        parts = call_kernel(
            functools.partial(text_grad_body, groups),
            [bf16(rows, width)] * groups,
            [place] + text_own + [acc_own, swap(acc_other, "blk", 1)],
            scalars=1,
            limit=16,
        )
        return [parts[0]] + [swap(parts[k], "tp", k) for k in range(1, groups)]

    def finish(text_parts, own, lows, highs):
        return call_kernel(
            functools.partial(finish_body, groups, len(lows), len(highs)),
            [bf16(groups * rows, width), bf16(rows)],
            [place] + text_parts + [image_emb, own] + lows + highs,
            scalars=1,
            limit=16,
        )

    if not square:
        spread, acc_own, acc_other = call_kernel(
            functools.partial(all_body, groups),
            [bf16(gathered.shape[0]), f32(rows), bf16(rows)],
            scalars + [place] + text_own + text_other + [gathered] + meta(sources),
            scalars=3,
            scratch=[
                pltpu.VMEM((both, embed), jnp.bfloat16),
                pltpu.VMEM(gathered.shape, jnp.bfloat16),
                pltpu.VMEM((both, gathered.shape[0]), jnp.bfloat16),
                pltpu.VMEM((both, embed), jnp.float32),
            ],
            limit=56,
        )
        text_parts = finish_text(acc_own, acc_other)
        parts = lax.all_to_all(
            spread, "blk", split_axis=0, concat_axis=0, tiled=True, axis_index_groups=same_core
        )
        total = jnp.sum(parts.reshape(-1, rows, embed).astype(jnp.float32), axis=0)
        return tuple(finish(text_parts, total, [], []))

    to_x_high, to_y_low, near_x_low, near_y_high, units, acc, own_weights = call_kernel(
        functools.partial(near_body, groups),
        [bf16(half), bf16(half), f32(half), f32(half), bf16(both), f32(both), bf16(both, rows)],
        scalars + [place] + text_own + text_other + [image_emb, from_x, from_y]
        + meta(sources[:3]),
        scalars=3,
        scratch=[
            pltpu.VMEM((3 * rows, embed), jnp.bfloat16),
            pltpu.VMEM((both, 3 * rows), jnp.bfloat16),
        ],
        flops=8 * unit_flops,
        transcendentals=2 * both * 3 * rows,
        limit=32,
    )
    from_x_high = swap(to_x_high, "blk", 2)
    from_y_low = swap(to_y_low, "blk", 4)
    far_low = swap(from_y[:half], "blk", 2)
    far_high = swap(from_x[half:], "blk", 4)
    to_far_low, to_far_high, acc_own, acc_other = call_kernel(
        far_body,
        [bf16(half), bf16(half), f32(rows), bf16(rows)],
        scalars + [units, acc, far_low, far_high] + meta(sources[3:]),
        scalars=2,
        scratch=[
            pltpu.VMEM((rows, embed), jnp.bfloat16),
            pltpu.VMEM((both, rows), jnp.bfloat16),
        ],
        flops=3 * unit_flops,
        transcendentals=2 * both * rows,
        limit=24,
    )
    relay_low = swap(to_far_low, "blk", 4)
    relay_high = swap(to_far_high, "blk", 2)
    text_parts = finish_text(acc_own, acc_other)
    own = call_kernel(own_body, [f32(rows)], [own_weights, units], flops=unit_flops, limit=16)[0]
    to_x_low, to_y_high = call_kernel(
        relay_body,
        [bf16(half), bf16(half)],
        [near_x_low, relay_low, near_y_high, relay_high],
        limit=16,
    )
    from_x_low = swap(to_x_low, "blk", 2)
    from_y_high = swap(to_y_high, "blk", 4)
    return tuple(
        finish(text_parts, own, [from_x_low, from_y_low], [from_x_high, from_y_high])
    )


def solution(mesh):
    in_specs = (P("blk", "tp"), P(("blk", "tp"), None), P(), P(), P(), P(), P())
    out_specs = (P("blk", "tp"), P(("blk", "tp"), None))
    return jax.shard_map(
        per_device, mesh=mesh, in_specs=in_specs, out_specs=out_specs, check_vma=False
    )
```

time: 488 us -> 82.3 us (0.17)
  the two profiles are of different devices: /device:TPU:0 before, /device:TPU:19 now
where the time goes in v2:
time: 82.3 us; the launch traced here: 81.7 us
  waiting for transfers between devices  30.8 us (37%)
  starting transfers between devices  19.9 us (24%)
  Pallas kernels  13.8 us (17%)
  local copies, waits for them, and re-layouts  12.1 us (15%)
  other arithmetic  3.02 us (4%)
  between operations  2.08 us (3%)
    ppermute x21, waiting for transfers between devices, swap(): return lax.ppermute(value, axis, [(i, i ^ bits) for i in range(count)])  30.8 us
    ppermute x21, starting transfers between devices, swap(): return lax.ppermute(value, axis, [(i, i ^ bits) for i in range(count)])  19.9 us
    pallas_call x6, Pallas kernels, call_kernel(): pl.pallas_call(body, out_shape=outs, in_specs=[SMEM_SPEC] * scalars + [VM...  13.8 us
    reduce_or x4, local copies, waits for them, and re-layouts, meta(): live = jnp.any(entries[:, None, :] == tile_range[None, :, None], axis=-1)  4 us
    unnamed x9, local copies, waits for them, and re-layouts  3.51 us
    dynamic_slice x1, local copies, waits for them, and re-layouts, text_rows(): return lax.dynamic_slice_in_dim(text_emb, (group ^ k) * rows, rows, 0)  2.01 us
  transfers between devices with their start and end apart: 21, of which 8 were waited for; matrix products, arithmetic and copies ran while one was open for 18% of the time, Pallas kernels for 11%

profile of v2, /device:TPU:19, one launch (start us, length us, event | category | flops | bytes accessed | tf_op | source)
XLA Modules:
  0.0 81.7 jit_solution(8079931442856940257)
XLA Ops:
  0.6 1.3 %collective-permute-start.8 = (bf16[384,1024]{1,0:T(8,128)(2,1)}, bf16[384,1024]{1,0:T(8,128)(2,1)S(1)}, u32[]{:S(2)}, u32[]{:S(2)}) collective-permute-start(bf16[384,1024]{1,0:T(8,128)(2,1)} %refs_5_.1), channel_id=1, source_target_pairs={{0,16},{4,20},{8,24},{12,28},{16,0},{20,4},{24,8},{28,12},{1,17},{... | collective-permute-start | bytes 2359304 | tf_op jit(solution)/shard_map/ppermute | solution.py:250
  1.9 0.3 collective-permute-start.7
  2.2 2.0 %constant_dynamic-slice_fusion.2 = (bf16[384,256]{1,0:T(8,128)(2,1)}, bf16[384,256]{1,0:T(8,128)(2,1)S(1)}, bf16[384,256]{1,0:T(8,128)(2,1)S(1)}, bf16[384,256]{1,0:T(8,128)(2,1)S(1)}) fusion(bf16[1536,256]{1,0:T(8,128)(2,1)} %param.7, s32[]{:T(128)S(6)} %select_n.69, s32[]{:T(128)S(6)} %select_n.67, s32[]{:T(128)S(6)} %select_n.66, s32[]{:T(128)S(6)} %select_n.68), kind=kLoop, calls=%fused_computation.30 | loop fusion | bytes 1572880 | tf_op jit(solution)/shard_map/dynamic_slice | solution.py:267
  4.4 1.1 %collective-permute-start = (bf16[384,256]{1,0:T(8,128)(2,1)S(1)}, bf16[384,256]{1,0:T(8,128)(2,1)S(1)}, u32[]{:S(2)}, u32[]{:S(2)}) collective-permute-start(bf16[384,256]{1,0:T(8,128)(2,1)S(1)} %get-tuple-element.37), channel_id=1, source_target_pairs={{0,1},{1,0},{2,3},{3,2},{4,5},{5,4},{6,7},{7,6},{8,9},{9,8},{10,11... | collective-permute-start | bytes 589832 | tf_op jit(solution)/shard_map/ppermute | solution.py:250
  5.5 2.1 %collective-permute-start.1 = (bf16[384,256]{1,0:T(8,128)(2,1)S(1)}, bf16[384,256]{1,0:T(8,128)(2,1)S(1)}, u32[]{:S(2)}, u32[]{:S(2)}) collective-permute-start(bf16[384,256]{1,0:T(8,128)(2,1)S(1)} %get-tuple-element.39), channel_id=1, source_target_pairs={{0,2},{1,3},{2,0},{3,1},{4,6},{5,7},{6,4},{7,5},{8,10},{9,11},{10,... | collective-permute-start | bytes 589832 | tf_op jit(solution)/shard_map/ppermute | solution.py:250
  8.9 0.9 %constant_dynamic-slice_fusion = (s32[3,8,3]{0,1,2:T(8,128)S(1)}, s32[3,8,3]{0,1,2:T(8,128)S(1)}) fusion(s32[96,8,3]{0,1,2:T(8,128)} %param.13, s32[]{:T(128)S(6)} %select_n.73, s32[]{:T(128)S(6)} %select_n.72), kind=kLoop, calls=%fused_computation.28 | loop fusion | bytes 1160 | tf_op jit(solution)/shard_map/dynamic_slice | solution.py:285
  9.8 0.7 fusion.4
  10.5 0.5 fusion.3
  11.0 1.3 %copy.20 = pred[6,3]{1,0:T(8,128)(4,1)} copy(pred[6,3]{0,1:T(4,128)(4,1)} %fusion.3) | data formatting | bytes 36 | tf_op jit(solution)/shard_map/reduce_or | solution.py:301
  12.3 0.5 fusion
  12.8 0.8 copy.17
  13.6 0.7 broadcast_bitcast_fusion.3
  14.2 0.7 copy.38
  14.9 0.5 fusion.1
  15.4 1.3 %copy.18 = pred[6,3]{1,0:T(8,128)(4,1)} copy(pred[6,3]{0,1:T(4,128)(4,1)} %fusion.1) | data formatting | bytes 36 | tf_op jit(solution)/shard_map/reduce_or | solution.py:301
  16.7 0.7 broadcast_bitcast_fusion.2
  17.5 0.7 copy.19
  18.2 0.7 broadcast_bitcast_fusion.1
  18.9 0.8 dynamic-slice_bitcast_fusion.1
  19.7 0.9 %fusion.8 = (s32[384]{0:T(512)S(1)}, s32[384]{0:T(512)S(1)}, s32[3,128]{1,0:T(4,128)S(1)}, s32[384]{0:T(512)S(1)}, s32[384]{0:T(512)S(1)}) fusion(s32[12288]{0:T(1024)} %param.11, s32[]{:T(128)S(6)} %select_n.83, s32[]{:T(128)S(6)} %select_n.77, s32[]{:T(128)S(6)} %select_n.71, s32[]{:T(128)S(6)} %select_n.70, s32[]{:T(128)S(6)} %select_n.80), kind=kLoop, calls=%fused_computation.49 | loop fusion | bytes 15380 | tf_op jit(solution)/shard_map/dynamic_slice | solution.py:282
  20.6 0.7 bitcast_select_fusion.3
  21.3 0.7 broadcast_bitcast_fusion
  22.0 1.8 %collective-permute-start.3 = (bf16[384,256]{1,0:T(8,128)(2,1)S(1)}, bf16[384,256]{1,0:T(8,128)(2,1)S(1)}, u32[]{:S(2)}, u32[]{:S(2)}) collective-permute-start(bf16[384,256]{1,0:T(8,128)(2,1)S(1)} %get-tuple-element.38.refs_3_.refs_1_), channel_id=1, source_target_pairs={{0,4},{4,0},{8,12},{12,8},{16,20},{20,16},{24,28},{28,24},{1,5},{5... | collective-permute-start | bytes 589832 | tf_op jit(solution)/shard_map/ppermute | solution.py:250
  23.9 0.4 collective-permute-start.4
  24.5 1.3 %collective-permute-start.9 = (bf16[192,1024]{1,0:T(8,128)(2,1)S(1)}, bf16[192,1024]{1,0:T(8,128)(2,1)S(1)}, u32[]{:S(2)}, u32[]{:S(2)}) collective-permute-start(bf16[192,1024]{1,0:T(8,128)(2,1)S(1)} %slice.8), channel_id=1, source_target_pairs={{0,8},{4,12},{8,0},{12,4},{16,24},{20,28},{24,16},{28,20},{1,9},{5... | collective-permute-start | bytes 1179656 | tf_op jit(solution)/shard_map/ppermute | solution.py:250
  25.8 0.3 collective-permute-start.10
  26.1 7.4 %shard_map.86 = (bf16[192,1024]{1,0:T(8,128)(2,1)S(1)}, bf16[192,1024]{1,0:T(8,128)(2,1)S(1)}, f32[192,1024]{1,0:T(8,128)S(1)}, f32[192,1024]{1,0:T(8,128)S(1)},...) custom-call(f32[1]{0:T(128)S(6)} %copy.39.refs_0_, f32[1]{0:T(128)S(6)} %copy.40.refs_1_, ...), custom_call_target="tpu_custom_call" | custom-call | flops 4831838208 | bytes 11638284 | tf_op jit(solution)/shard_map/pallas_call | solution.py:25
  33.5 1.3 %collective-permute-done.9.refs_4_ = bf16[192,1024]{1,0:T(8,128)(2,1)S(1)} collective-permute-done((bf16[192,1024]{1,0:T(8,128)(2,1)S(1)}, bf16[192,1024]{1,0:T(8,128)(2,1)S(1)}, u32[]{:S(2)}, u32[]{:S(2)}) %collective-permute-start.9) | collective-permute-done | bytes 393248 | tf_op jit(solution)/shard_map/ppermute | solution.py:250
  34.8 1.0 %collective-permute-done.10.refs_5_ = bf16[192,1024]{1,0:T(8,128)(2,1)S(1)} collective-permute-done((bf16[192,1024]{1,0:T(8,128)(2,1)S(1)}, bf16[192,1024]{1,0:T(8,128)(2,1)S(1)}, u32[]{:S(2)}, u32[]{:S(2)}) %collective-permute-start.10) | collective-permute-done | bytes 393248 | tf_op jit(solution)/shard_map/ppermute | solution.py:250
  35.8 2.9 %shard_map.87 = (bf16[192,1024]{1,0:T(8,128)(2,1)S(1)}, bf16[192,1024]{1,0:T(8,128)(2,1)S(1)}, f32[384,1024]{1,0:T(8,128)S(1)}, bf16[384,1024]{1,0:T(8,128)(2,1)S(1)}) custom-call(f32[1]{0:T(128)S(6)} %copy.39.refs_0_, f32[1]{0:T(128)S(6)} %copy.40.refs_1_, bf16[768,1024]{1,0:T(8,128)(2,1)S(1)} %get-tuple-element.19.refs_2_.unit_ref, ...), custom_call_target="tpu_custom_call" | custom-call | flops 1811939328 | bytes 8667656 | tf_op jit(solution)/shard_map/pallas_call | solution.py:25
  38.7 1.6 %collective-permute-start.11 = (bf16[384,1024]{1,0:T(8,128)(2,1)S(1)}, bf16[384,1024]{1,0:T(8,128)(2,1)S(1)}, u32[]{:S(2)}, u32[]{:S(2)}) collective-permute-start(bf16[384,1024]{1,0:T(8,128)(2,1)S(1)} %get-tuple-element.22), channel_id=1, source_target_pairs={{0,4},{4,0},{8,12},{12,8},{16,20},{20,16},{24,28},{28,24},{1,5},{5... | collective-permute-start | bytes 2359304 | tf_op jit(solution)/shard_map/ppermute | solution.py:250
  40.3 0.2 collective-permute-start.15
  40.6 0.2 collective-permute-start.16
  40.8 1.2 %collective-permute-start.18 = (bf16[192,1024]{1,0:T(8,128)(2,1)S(1)}, bf16[192,1024]{1,0:T(8,128)(2,1)S(1)}, u32[]{:S(2)}, u32[]{:S(2)}) collective-permute-start(bf16[192,1024]{1,0:T(8,128)(2,1)S(1)} %get-tuple-element.33), channel_id=1, source_target_pairs={{0,16},{4,20},{8,24},{12,28},{16,0},{20,4},{24,8},{28,12},{1,17},{... | collective-permute-start | bytes 1179656 | tf_op jit(solution)/shard_map/ppermute | solution.py:250
  42.1 1.2 %collective-permute-start.19 = (bf16[192,1024]{1,0:T(8,128)(2,1)S(1)}, bf16[192,1024]{1,0:T(8,128)(2,1)S(1)}, u32[]{:S(2)}, u32[]{:S(2)}) collective-permute-start(bf16[192,1024]{1,0:T(8,128)(2,1)S(1)} %get-tuple-element.34), channel_id=1, source_target_pairs={{0,8},{4,12},{8,0},{12,4},{16,24},{20,28},{24,16},{28,20},{1,9},{5... | collective-permute-start | bytes 1179656 | tf_op jit(solution)/shard_map/ppermute | solution.py:250
  43.3 7.7 %collective-permute-done.15.left_in_ref = bf16[192,1024]{1,0:T(8,128)(2,1)S(1)} collective-permute-done((bf16[192,1024]{1,0:T(8,128)(2,1)S(1)}, bf16[192,1024]{1,0:T(8,128)(2,1)S(1)}, u32[]{:S(2)}, u32[]{:S(2)}) %collective-permute-start.15) | collective-permute-done | bytes 393248 | tf_op jit(solution)/shard_map/ppermute | solution.py:250
  51.2 0.3 collective-permute-start.17
  51.5 1.1 %collective-permute-start.20 = (bf16[192,1024]{1,0:T(8,128)(2,1)S(1)}, bf16[192,1024]{1,0:T(8,128)(2,1)S(1)}, u32[]{:S(2)}, u32[]{:S(2)}) collective-permute-start(bf16[192,1024]{1,0:T(8,128)(2,1)S(1)} %get-tuple-element.35), channel_id=1, source_target_pairs={{0,16},{4,20},{8,24},{12,28},{16,0},{20,4},{24,8},{28,12},{1,17},{... | collective-permute-start | bytes 1179656 | tf_op jit(solution)/shard_map/ppermute | solution.py:250
  52.6 0.8 shard_map.88
  53.4 1.9 %collective-permute-start.12 = (bf16[384,256]{1,0:T(8,128)(2,1)S(1)}, bf16[384,256]{1,0:T(8,128)(2,1)S(1)}, u32[]{:S(2)}, u32[]{:S(2)}) collective-permute-start(bf16[384,256]{1,0:T(8,128)(2,1)S(1)} %get-tuple-element.24), channel_id=1, source_target_pairs={{0,1},{1,0},{2,3},{3,2},{4,5},{5,4},{6,7},{7,6},{8,9},{9,8},{10,11... | collective-permute-start | bytes 589832 | tf_op jit(solution)/shard_map/ppermute | solution.py:250
  55.3 4.2 %collective-permute-done.18.refs_8_ = bf16[192,1024]{1,0:T(8,128)(2,1)S(1)} collective-permute-done((bf16[192,1024]{1,0:T(8,128)(2,1)S(1)}, bf16[192,1024]{1,0:T(8,128)(2,1)S(1)}, u32[]{:S(2)}, u32[]{:S(2)}) %collective-permute-start.18) | collective-permute-done | bytes 393248 | tf_op jit(solution)/shard_map/ppermute | solution.py:250
  59.5 1.0 %collective-permute-start.13 = (bf16[384,256]{1,0:T(8,128)(2,1)S(1)}, bf16[384,256]{1,0:T(8,128)(2,1)S(1)}, u32[]{:S(2)}, u32[]{:S(2)}) collective-permute-start(bf16[384,256]{1,0:T(8,128)(2,1)S(1)} %get-tuple-element.25), channel_id=1, source_target_pairs={{0,2},{1,3},{2,0},{3,1},{4,6},{5,7},{6,4},{7,5},{8,10},{9,11},{10,... | collective-permute-start | bytes 589832 | tf_op jit(solution)/shard_map/ppermute | solution.py:250
  60.5 2.0 %collective-permute-start.14 = (bf16[384,256]{1,0:T(8,128)(2,1)S(1)}, bf16[384,256]{1,0:T(8,128)(2,1)S(1)}, u32[]{:S(2)}, u32[]{:S(2)}) collective-permute-start(bf16[384,256]{1,0:T(8,128)(2,1)S(1)} %get-tuple-element.26), channel_id=1, source_target_pairs={{0,3},{1,2},{2,1},{3,0},{4,7},{5,6},{6,5},{7,4},{8,11},{9,10},{10,... | collective-permute-start | bytes 589832 | tf_op jit(solution)/shard_map/ppermute | solution.py:250
  62.5 0.8 shard_map.89.refs_6_
  63.3 4.5 %collective-permute-done.17.refs_7_ = bf16[192,1024]{1,0:T(8,128)(2,1)S(1)} collective-permute-done((bf16[192,1024]{1,0:T(8,128)(2,1)S(1)}, bf16[192,1024]{1,0:T(8,128)(2,1)S(1)}, u32[]{:S(2)}, u32[]{:S(2)}) %collective-permute-start.17) | collective-permute-done | bytes 393248 | tf_op jit(solution)/shard_map/ppermute | solution.py:250
  67.9 5.1 %collective-permute-done.13.refs_3_ = bf16[384,256]{1,0:T(8,128)(2,1)S(1)} collective-permute-done((bf16[384,256]{1,0:T(8,128)(2,1)S(1)}, bf16[384,256]{1,0:T(8,128)(2,1)S(1)}, u32[]{:S(2)}, u32[]{:S(2)}) %collective-permute-start.13) | collective-permute-done | bytes 196640 | tf_op jit(solution)/shard_map/ppermute | solution.py:250
  73.0 6.9 %collective-permute-done.14.refs_4_ = bf16[384,256]{1,0:T(8,128)(2,1)S(1)} collective-permute-done((bf16[384,256]{1,0:T(8,128)(2,1)S(1)}, bf16[384,256]{1,0:T(8,128)(2,1)S(1)}, u32[]{:S(2)}, u32[]{:S(2)}) %collective-permute-start.14) | collective-permute-done | bytes 196640 | tf_op jit(solution)/shard_map/ppermute | solution.py:250
  79.8 1.8 %shard_map.91 = (bf16[1536,256]{1,0:T(8,128)(2,1)}, bf16[384,1024]{1,0:T(8,128)(2,1)}) custom-call(s32[1]{0:T(128)} %bitcast.refs_2_.refs_0_, bf16[384,256]{1,0:T(8,128)(2,1)S(1)} %get-tuple-element.23.refs_1_, bf16[384,256]{1,0:T(8,128)(2,1)S(1)} %collective-permute-done.12.refs_2_, bf16[384,256]{1,0:T(8,128)(2,1)S(1)} %collective-permute-done.13.refs_3_, ...), custom_call_target="tpu_custom_call" | custom-call | bytes 6291460 | tf_op jit(solution)/shard_map/pallas_call | solution.py:25
  (34 shorter events, 0.7 us)
Async XLA Ops:
  0.6 23.7 %collective-permute-start.8 = (bf16[384,1024]{1,0:T(8,128)(2,1)}, bf16[384,1024]{1,0:T(8,128)(2,1)S(1)}, u32[]{:S(2)}, u32[]{:S(2)}) collective-permute-start(bf16[384,1024]{1,0:T(8,128)(2,1)} %refs_5_.1), channel_id=1, source_target_pairs={{0,16},{4,20},{8,24},{12,28},{16,0},{20,4},{24,8},{28,12},{1,17},{... | collective-permute-start | bytes 2359304 | tf_op jit(solution)/shard_map/ppermute | solution.py:250
  1.9 22.5 %collective-permute-start.7 = (bf16[384,1024]{1,0:T(8,128)(2,1)}, bf16[384,1024]{1,0:T(8,128)(2,1)S(1)}, u32[]{:S(2)}, u32[]{:S(2)}) collective-permute-start(bf16[384,1024]{1,0:T(8,128)(2,1)} %refs_5_.1), channel_id=1, source_target_pairs={{0,8},{4,12},{8,0},{12,4},{16,24},{20,28},{24,16},{28,20},{1,9},{5... | collective-permute-start | bytes 2359304 | tf_op jit(solution)/shard_map/ppermute | solution.py:250
  2.2 23.9 %copy-start = (bf16[384,1024]{1,0:T(8,128)(2,1)S(1)}, bf16[384,1024]{1,0:T(8,128)(2,1)}, u32[]{:S(2)}) copy-start(bf16[384,1024]{1,0:T(8,128)(2,1)} %refs_5_.1) | copy-start | bytes 2359300
  4.2 17.8 %collective-permute-start.2 = (bf16[384,256]{1,0:T(8,128)(2,1)}, bf16[384,256]{1,0:T(8,128)(2,1)S(1)}, u32[]{:S(2)}, u32[]{:S(2)}) collective-permute-start(bf16[384,256]{1,0:T(8,128)(2,1)} %get-tuple-element.36), channel_id=1, source_target_pairs={{0,3},{1,2},{2,1},{3,0},{4,7},{5,6},{6,5},{7,4},{8,11},{9,10},{10,... | collective-permute-start | bytes 589832 | tf_op jit(solution)/shard_map/ppermute | solution.py:250
  4.4 19.5 %collective-permute-start = (bf16[384,256]{1,0:T(8,128)(2,1)S(1)}, bf16[384,256]{1,0:T(8,128)(2,1)S(1)}, u32[]{:S(2)}, u32[]{:S(2)}) collective-permute-start(bf16[384,256]{1,0:T(8,128)(2,1)S(1)} %get-tuple-element.37), channel_id=1, source_target_pairs={{0,1},{1,0},{2,3},{3,2},{4,5},{5,4},{6,7},{7,6},{8,9},{9,8},{10,11... | collective-permute-start | bytes 589832 | tf_op jit(solution)/shard_map/ppermute | solution.py:250
  5.5 18.4 %collective-permute-start.1 = (bf16[384,256]{1,0:T(8,128)(2,1)S(1)}, bf16[384,256]{1,0:T(8,128)(2,1)S(1)}, u32[]{:S(2)}, u32[]{:S(2)}) collective-permute-start(bf16[384,256]{1,0:T(8,128)(2,1)S(1)} %get-tuple-element.39), channel_id=1, source_target_pairs={{0,2},{1,3},{2,0},{3,1},{4,6},{5,7},{6,4},{7,5},{8,10},{9,11},{10,... | collective-permute-start | bytes 589832 | tf_op jit(solution)/shard_map/ppermute | solution.py:250
  22.0 3.8 %collective-permute-start.3 = (bf16[384,256]{1,0:T(8,128)(2,1)S(1)}, bf16[384,256]{1,0:T(8,128)(2,1)S(1)}, u32[]{:S(2)}, u32[]{:S(2)}) collective-permute-start(bf16[384,256]{1,0:T(8,128)(2,1)S(1)} %get-tuple-element.38.refs_3_.refs_1_), channel_id=1, source_target_pairs={{0,4},{4,0},{8,12},{12,8},{16,20},{20,16},{24,28},{28,24},{1,5},{5... | collective-permute-start | bytes 589832 | tf_op jit(solution)/shard_map/ppermute | solution.py:250
  23.8 2.3 %collective-permute-start.6 = (bf16[384,256]{1,0:T(8,128)(2,1)S(1)}, bf16[384,256]{1,0:T(8,128)(2,1)S(1)}, u32[]{:S(2)}, u32[]{:S(2)}) collective-permute-start(bf16[384,256]{1,0:T(8,128)(2,1)S(1)} %collective-permute-done.2.refs_6_.refs_4_), channel_id=1, source_target_pairs={{0,4},{4,0},{8,12},{12,8},{16,20},{20,16},{24,28},{28,24},{1,5},{5... | collective-permute-start | bytes 589832 | tf_op jit(solution)/shard_map/ppermute | solution.py:250
  23.9 2.2 %collective-permute-start.4 = (bf16[384,256]{1,0:T(8,128)(2,1)S(1)}, bf16[384,256]{1,0:T(8,128)(2,1)S(1)}, u32[]{:S(2)}, u32[]{:S(2)}) collective-permute-start(bf16[384,256]{1,0:T(8,128)(2,1)S(1)} %collective-permute-done.refs_4_.refs_2_), channel_id=1, source_target_pairs={{0,4},{4,0},{8,12},{12,8},{16,20},{20,16},{24,28},{28,24},{1,5},{5... | collective-permute-start | bytes 589832 | tf_op jit(solution)/shard_map/ppermute | solution.py:250
  24.3 1.8 %collective-permute-start.5 = (bf16[384,256]{1,0:T(8,128)(2,1)S(1)}, bf16[384,256]{1,0:T(8,128)(2,1)S(1)}, u32[]{:S(2)}, u32[]{:S(2)}) collective-permute-start(bf16[384,256]{1,0:T(8,128)(2,1)S(1)} %collective-permute-done.1.refs_5_.refs_3_), channel_id=1, source_target_pairs={{0,4},{4,0},{8,12},{12,8},{16,20},{20,16},{24,28},{28,24},{1,5},{5... | collective-permute-start | bytes 589832 | tf_op jit(solution)/shard_map/ppermute | solution.py:250
  24.5 10.3 %collective-permute-start.9 = (bf16[192,1024]{1,0:T(8,128)(2,1)S(1)}, bf16[192,1024]{1,0:T(8,128)(2,1)S(1)}, u32[]{:S(2)}, u32[]{:S(2)}) collective-permute-start(bf16[192,1024]{1,0:T(8,128)(2,1)S(1)} %slice.8), channel_id=1, source_target_pairs={{0,8},{4,12},{8,0},{12,4},{16,24},{20,28},{24,16},{28,20},{1,9},{5... | collective-permute-start | bytes 1179656 | tf_op jit(solution)/shard_map/ppermute | solution.py:250
  25.8 10.0 %collective-permute-start.10 = (bf16[192,1024]{1,0:T(8,128)(2,1)S(1)}, bf16[192,1024]{1,0:T(8,128)(2,1)S(1)}, u32[]{:S(2)}, u32[]{:S(2)}) collective-permute-start(bf16[192,1024]{1,0:T(8,128)(2,1)S(1)} %slice.9), channel_id=1, source_target_pairs={{0,16},{4,20},{8,24},{12,28},{16,0},{20,4},{24,8},{28,12},{1,17},{... | collective-permute-start | bytes 1179656 | tf_op jit(solution)/shard_map/ppermute | solution.py:250
  38.7 13.9 %collective-permute-start.11 = (bf16[384,1024]{1,0:T(8,128)(2,1)S(1)}, bf16[384,1024]{1,0:T(8,128)(2,1)S(1)}, u32[]{:S(2)}, u32[]{:S(2)}) collective-permute-start(bf16[384,1024]{1,0:T(8,128)(2,1)S(1)} %get-tuple-element.22), channel_id=1, source_target_pairs={{0,4},{4,0},{8,12},{12,8},{16,20},{20,16},{24,28},{28,24},{1,5},{5... | collective-permute-start | bytes 2359304 | tf_op jit(solution)/shard_map/ppermute | solution.py:250
  40.3 10.7 %collective-permute-start.15 = (bf16[192,1024]{1,0:T(8,128)(2,1)S(1)}, bf16[192,1024]{1,0:T(8,128)(2,1)S(1)}, u32[]{:S(2)}, u32[]{:S(2)}) collective-permute-start(bf16[192,1024]{1,0:T(8,128)(2,1)S(1)} %get-tuple-element.29), channel_id=1, source_target_pairs={{0,16},{4,20},{8,24},{12,28},{16,0},{20,4},{24,8},{28,12},{1,17},{... | collective-permute-start | bytes 1179656 | tf_op jit(solution)/shard_map/ppermute | solution.py:250
  40.6 10.5 %collective-permute-start.16 = (bf16[192,1024]{1,0:T(8,128)(2,1)S(1)}, bf16[192,1024]{1,0:T(8,128)(2,1)S(1)}, u32[]{:S(2)}, u32[]{:S(2)}) collective-permute-start(bf16[192,1024]{1,0:T(8,128)(2,1)S(1)} %get-tuple-element.31), channel_id=1, source_target_pairs={{0,8},{4,12},{8,0},{12,4},{16,24},{20,28},{24,16},{28,20},{1,9},{5... | collective-permute-start | bytes 1179656 | tf_op jit(solution)/shard_map/ppermute | solution.py:250
  40.8 18.6 %collective-permute-start.18 = (bf16[192,1024]{1,0:T(8,128)(2,1)S(1)}, bf16[192,1024]{1,0:T(8,128)(2,1)S(1)}, u32[]{:S(2)}, u32[]{:S(2)}) collective-permute-start(bf16[192,1024]{1,0:T(8,128)(2,1)S(1)} %get-tuple-element.33), channel_id=1, source_target_pairs={{0,16},{4,20},{8,24},{12,28},{16,0},{20,4},{24,8},{28,12},{1,17},{... | collective-permute-start | bytes 1179656 | tf_op jit(solution)/shard_map/ppermute | solution.py:250
  42.1 18.4 %collective-permute-start.19 = (bf16[192,1024]{1,0:T(8,128)(2,1)S(1)}, bf16[192,1024]{1,0:T(8,128)(2,1)S(1)}, u32[]{:S(2)}, u32[]{:S(2)}) collective-permute-start(bf16[192,1024]{1,0:T(8,128)(2,1)S(1)} %get-tuple-element.34), channel_id=1, source_target_pairs={{0,8},{4,12},{8,0},{12,4},{16,24},{20,28},{24,16},{28,20},{1,9},{5... | collective-permute-start | bytes 1179656 | tf_op jit(solution)/shard_map/ppermute | solution.py:250
  51.2 16.6 %collective-permute-start.17 = (bf16[192,1024]{1,0:T(8,128)(2,1)S(1)}, bf16[192,1024]{1,0:T(8,128)(2,1)S(1)}, u32[]{:S(2)}, u32[]{:S(2)}) collective-permute-start(bf16[192,1024]{1,0:T(8,128)(2,1)S(1)} %get-tuple-element.32), channel_id=1, source_target_pairs={{0,8},{4,12},{8,0},{12,4},{16,24},{20,28},{24,16},{28,20},{1,9},{5... | collective-permute-start | bytes 1179656 | tf_op jit(solution)/shard_map/ppermute | solution.py:250
  51.5 16.4 %collective-permute-start.20 = (bf16[192,1024]{1,0:T(8,128)(2,1)S(1)}, bf16[192,1024]{1,0:T(8,128)(2,1)S(1)}, u32[]{:S(2)}, u32[]{:S(2)}) collective-permute-start(bf16[192,1024]{1,0:T(8,128)(2,1)S(1)} %get-tuple-element.35), channel_id=1, source_target_pairs={{0,16},{4,20},{8,24},{12,28},{16,0},{20,4},{24,8},{28,12},{1,17},{... | collective-permute-start | bytes 1179656 | tf_op jit(solution)/shard_map/ppermute | solution.py:250
  53.4 14.5 %collective-permute-start.12 = (bf16[384,256]{1,0:T(8,128)(2,1)S(1)}, bf16[384,256]{1,0:T(8,128)(2,1)S(1)}, u32[]{:S(2)}, u32[]{:S(2)}) collective-permute-start(bf16[384,256]{1,0:T(8,128)(2,1)S(1)} %get-tuple-element.24), channel_id=1, source_target_pairs={{0,1},{1,0},{2,3},{3,2},{4,5},{5,4},{6,7},{7,6},{8,9},{9,8},{10,11... | collective-permute-start | bytes 589832 | tf_op jit(solution)/shard_map/ppermute | solution.py:250
  59.5 13.5 %collective-permute-start.13 = (bf16[384,256]{1,0:T(8,128)(2,1)S(1)}, bf16[384,256]{1,0:T(8,128)(2,1)S(1)}, u32[]{:S(2)}, u32[]{:S(2)}) collective-permute-start(bf16[384,256]{1,0:T(8,128)(2,1)S(1)} %get-tuple-element.25), channel_id=1, source_target_pairs={{0,2},{1,3},{2,0},{3,1},{4,6},{5,7},{6,4},{7,5},{8,10},{9,11},{10,... | collective-permute-start | bytes 589832 | tf_op jit(solution)/shard_map/ppermute | solution.py:250
  60.5 19.3 %collective-permute-start.14 = (bf16[384,256]{1,0:T(8,128)(2,1)S(1)}, bf16[384,256]{1,0:T(8,128)(2,1)S(1)}, u32[]{:S(2)}, u32[]{:S(2)}) collective-permute-start(bf16[384,256]{1,0:T(8,128)(2,1)S(1)} %get-tuple-element.26), channel_id=1, source_target_pairs={{0,3},{1,2},{2,1},{3,0},{4,7},{5,6},{6,5},{7,4},{8,11},{9,10},{10,... | collective-permute-start | bytes 589832 | tf_op jit(solution)/shard_map/ppermute | solution.py:250

commit v3 on v0

v3 whole, which is shorter than its diff:
```python
import functools
import math

import jax
import jax.numpy as jnp
from jax import lax
from jax.experimental import pallas as pl
from jax.experimental.pallas import tpu as pltpu
from jax.sharding import PartitionSpec as P

TILE = 128
SLOTS = 3
WAIT_FLOPS = 20_000_000_000
TEXT_PIECES = 2
LAST_PIECES = 1
CORES = 2
EPS = 1e-06
LOG2E = math.log2(math.e)
MIB = 1024 * 1024

VMEM_SPEC = pl.BlockSpec(memory_space=pltpu.VMEM)
SMEM_SPEC = pl.BlockSpec(memory_space=pltpu.SMEM)


def call_kernel(
    body, outs, operands, scalars=0, anywhere=(), scratch=(), flops=0, transcendentals=0, limit=24
):
    moved = sum(x.size * x.dtype.itemsize for x in operands)
    moved += sum(math.prod(o.shape) * o.dtype.itemsize for o in outs)
    specs = [SMEM_SPEC] * scalars + [VMEM_SPEC] * (len(operands) - scalars)
    for at in anywhere:
        specs[at] = pl.BlockSpec(memory_space=pl.ANY)
    return pl.pallas_call(
        body,
        out_shape=outs,
        in_specs=specs,
        out_specs=[VMEM_SPEC] * len(outs),
        scratch_shapes=list(scratch),
        compiler_params=pltpu.CompilerParams(vmem_limit_bytes=limit * MIB),
        cost_estimate=pl.CostEstimate(
            flops=flops, bytes_accessed=moved, transcendentals=transcendentals
        ),
    )(*operands)


def struct(shape, dtype):
    return jax.ShapeDtypeStruct(shape, dtype)


def row_scales(square_sum):
    return lax.rsqrt(square_sum + EPS)


def column_of(row):
    return jnp.broadcast_to(row, (TILE, TILE)).T


def dot_nt(left, right):
    return lax.dot_general(
        left, right, (((1,), (1,)), ((), ())), preferred_element_type=jnp.float32
    )


def dot_tn(left, right):
    return lax.dot_general(
        left, right, (((0,), (0,)), ((), ())), preferred_element_type=jnp.float32
    )


def feature_slice(place, k, width):
    return pl.ds(pl.multiple_of((place ^ k) * width, width), width)


def pick_body(where_ref, text_ref, *refs):
    out_refs, sems = refs[:-1], refs[-1]
    place = where_ref[1]
    rows = out_refs[0].shape[0]
    copies = []
    for k in list(range(1, len(out_refs))) + [0]:
        block = pl.ds(pl.multiple_of((place ^ k) * rows, rows), rows)
        copies.append(pltpu.make_async_copy(text_ref.at[block, :], out_refs[k], sems.at[k]))
    for copy in copies:
        copy.start()
    for copy in copies:
        copy.wait()


def unit_text_body(chunks, *refs):
    where_ref, chunk_refs, unit_ref = refs[0], refs[1 : 1 + chunks], refs[1 + chunks]
    piece_refs = refs[2 + chunks :]
    place = where_ref[1]
    rows, width = chunk_refs[0].shape
    for first in range(0, rows, TILE):
        part = pl.ds(first, TILE)
        parts = [ref[part, :].astype(jnp.float32) for ref in chunk_refs]
        scales = row_scales(sum(jnp.sum(x * x, axis=-1, keepdims=True) for x in parts))
        for k, x in enumerate(parts):
            unit_ref[part, feature_slice(place, k, width)] = (x * scales).astype(jnp.bfloat16)
    split_rows(unit_ref, piece_refs)


def split_rows(whole_ref, piece_refs):
    for at, ref in enumerate(piece_refs):
        ref[...] = whole_ref[pl.ds(at * ref.shape[0], ref.shape[0]), :]


def join_rows(piece_refs, whole_ref):
    for at, ref in enumerate(piece_refs):
        whole_ref[pl.ds(at * ref.shape[0], ref.shape[0]), :] = ref[...]


def unit_images(piece_refs, image_ref):
    start = 0
    step = 64
    for ref in piece_refs:
        for first in range(0, ref.shape[0], step):
            values = ref[pl.ds(first, step), :].astype(jnp.float32)
            scales = row_scales(jnp.sum(values * values, axis=-1, keepdims=True))
            image_ref[pl.ds(start + first, step), :] = (values * scales).astype(jnp.bfloat16)
        start += ref.shape[0]


def unit_images_body(*refs):
    unit_images(refs[:-1], refs[-1])


def neighbour_bits(shard):
    core = shard % CORES
    return 2 << core, 4 >> core


class Pairs:
    count = 6

    def __init__(self, refs, groups, tiles):
        self.scale_ref, self.bias_ref, self.where_ref, self.blocks_ref = refs[:4]
        self.bucket_ref, self.positive_ref = refs[4:6]
        self.groups, self.tiles = groups, tiles
        self.here, self.place = self.where_ref[0], self.where_ref[1]
        self.first_bit, self.second_bit = neighbour_bits(self.here)
        self.scale = self.scale_ref[0]
        self.slope = -self.scale * LOG2E
        self.offset = -self.bias_ref[0] * LOG2E

    def first_tile(self, shard):
        return (shard * self.groups + self.place) * self.tiles

    def weigh(self, products, text_shard, image_shard, weight_ref, top, left, own):
        text_tile = self.first_tile(text_shard)
        image_tile = self.first_tile(image_shard)
        for a in range(self.tiles):
            tile = text_tile + a
            row_bucket = column_of(self.bucket_ref[pl.ds(tile, 1), :])
            entries = [self.blocks_ref[slot, image_shard, tile] for slot in range(SLOTS)]
            for j in range(self.tiles):
                listed = sum(jnp.where(entry == j, 1.0, 0.0) for entry in entries)
                amount = self.scale * listed
                column_bucket = self.bucket_ref[pl.ds(image_tile + j, 1), :]
                power = (
                    products[a * TILE : (a + 1) * TILE, j * TILE : (j + 1) * TILE] * self.slope
                    + self.offset
                )
                factor = jnp.where(row_bucket == column_bucket, amount, 0.0)
                if own == "search" or (own == "diagonal" and a == j):
                    ids = lax.broadcasted_iota(jnp.int32, (1, TILE), 1) + (image_tile + j) * TILE
                    matched = column_of(self.positive_ref[pl.ds(tile, 1), :]) == ids
                    power = jnp.where(matched, -power, power)
                    factor = jnp.where(matched, -amount, factor)
                below = 1.0 + jnp.exp2(power)
                inverse = pl.reciprocal(below, approx=True)
                inverse = inverse * (2.0 - below * inverse)
                weight_ref[pl.ds(top + a * TILE, TILE), pl.ds(left + j * TILE, TILE)] = (
                    factor * inverse
                ).astype(jnp.bfloat16)


def near_pairs(pairs, text_shard, own, unit_ref, image_ref, weight_ref, acc_ref, own_weight_ref):
    rows = unit_ref.shape[0]
    order = (1, 2, 0)
    shards = (pairs.here, pairs.here ^ pairs.first_bit, pairs.here ^ pairs.second_bit)
    group = [pl.ds(q * rows, rows) for q in range(3)]
    totals = []
    products = dot_nt(unit_ref[...], image_ref[group[order[0]], :])
    for at, q in enumerate(order):
        now = products
        if at + 1 < len(order):
            products = dot_nt(unit_ref[...], image_ref[group[order[at + 1]], :])
        pairs.weigh(now, text_shard, shards[q], weight_ref, 0, q * rows, own if q == 0 else None)
        if q == 0:
            own_weight_ref[...] = weight_ref[:, group[0]]
        else:
            totals.append(dot_tn(weight_ref[:, group[q]], unit_ref[...]))
    acc_ref[...] = jnp.dot(weight_ref[...], image_ref[...], preferred_element_type=jnp.float32)
    return totals


def near_own_body(groups, tiles, *refs):
    pairs = Pairs(refs, groups, tiles)
    unit_ref, image_ref, first_ref, second_ref, acc_ref, own_weight_ref, weight_ref = refs[
        Pairs.count :
    ]
    totals = near_pairs(
        pairs, pairs.here, "diagonal", unit_ref, image_ref, weight_ref, acc_ref, own_weight_ref
    )
    first_ref[...], second_ref[...] = totals


def near_other_body(groups, tiles, *refs):
    pairs = Pairs(refs, groups, tiles)
    piece_refs = refs[Pairs.count : Pairs.count + TEXT_PIECES]
    refs = refs[Pairs.count + TEXT_PIECES :]
    image_ref, first_in_ref, second_in_ref = refs[:3]
    unit_ref, first_ref, second_ref, acc_ref, own_weight_ref, weight_ref = refs[3:]
    join_rows(piece_refs, unit_ref)
    first, second = near_pairs(
        pairs, pairs.here ^ 1, None, unit_ref, image_ref, weight_ref, acc_ref, own_weight_ref
    )
    first_ref[...] = (first + first_in_ref[...]).astype(jnp.bfloat16)
    second_ref[...] = second + second_in_ref[...]


def far_body(groups, tiles, *refs):
    pairs = Pairs(refs, groups, tiles)
    own_ref, other_ref, acc_own_in_ref, acc_other_in_ref = refs[Pairs.count : Pairs.count + 4]
    piece_ref = refs[Pairs.count + 4]
    acc_other_ref, acc_own_ref, far_ref, image_ref, weight_ref = refs[Pairs.count + 5 :]
    shard = pairs.here ^ 6
    unit_images([piece_ref], image_ref)
    other_products = dot_nt(other_ref[...], image_ref[...])
    own_products = dot_nt(own_ref[...], image_ref[...])
    pairs.weigh(other_products, pairs.here ^ 1, shard, weight_ref, 0, 0, None)
    weights = weight_ref[...]
    acc_other_ref[...] = (
        acc_other_in_ref[...]
        + jnp.dot(weights, image_ref[...], preferred_element_type=jnp.float32)
    ).astype(jnp.bfloat16)
    total = dot_tn(weights, other_ref[...])
    pairs.weigh(own_products, pairs.here, shard, weight_ref, 0, 0, None)
    weights = weight_ref[...]
    acc_own_ref[...] = acc_own_in_ref[...] + jnp.dot(
        weights, image_ref[...], preferred_element_type=jnp.float32
    )
    far_ref[...] = (total + dot_tn(weights, own_ref[...])).astype(jnp.bfloat16)


def own_sum_body(own_weight_ref, own_ref, other_weight_ref, other_ref, out_ref):
    out_ref[...] = dot_tn(own_weight_ref[...], own_ref[...]) + dot_tn(
        other_weight_ref[...], other_ref[...]
    )


def widen_body(in_ref, out_ref):
    out_ref[...] = in_ref[...].astype(jnp.float32)


def all_body(groups, tiles, chips, *refs):
    pairs = Pairs(refs, groups, tiles)
    own_ref, other_ref, piece_ref = refs[Pairs.count : Pairs.count + 3]
    spread_ref, acc_own_ref, acc_other_ref, image_ref, weight_ref = refs[Pairs.count + 3 :]
    rows = own_ref.shape[0]
    unit_images([piece_ref], image_ref)
    for text_ref, shard, top, own in (
        (own_ref, pairs.here, 0, "search"),
        (other_ref, pairs.here ^ 1, rows, None),
    ):
        for chip in range(chips):
            products = dot_nt(text_ref[...], image_ref[pl.ds(chip * rows, rows), :])
            image_shard = chip * CORES + pairs.here % CORES
            pairs.weigh(products, shard, image_shard, weight_ref, top, chip * rows, own)
        acc = jnp.dot(
            weight_ref[pl.ds(top, rows), :], image_ref[...], preferred_element_type=jnp.float32
        )
        if top == 0:
            acc_own_ref[...] = acc
        else:
            acc_other_ref[...] = acc.astype(jnp.bfloat16)
    for chip in range(chips):
        columns = pl.ds(chip * rows, rows)
        total = dot_tn(weight_ref[pl.ds(0, rows), columns], own_ref[...])
        total += dot_tn(weight_ref[pl.ds(rows, rows), columns], other_ref[...])
        spread_ref[columns, :] = total.astype(jnp.bfloat16)


def relay_body(sum_ref, in_ref, *out_refs):
    for at, ref in enumerate(out_refs):
        part = pl.ds(at * ref.shape[0], ref.shape[0])
        ref[...] = (sum_ref[part, :] + in_ref[part, :].astype(jnp.float32)).astype(jnp.bfloat16)


def text_grad_body(chunks, *refs):
    where_ref = refs[0]
    raw_refs = refs[1 : 1 + chunks]
    acc_ref, add_ref = refs[1 + chunks : 3 + chunks]
    out_refs = refs[3 + chunks :]
    place = where_ref[1]
    rows, width = raw_refs[0].shape
    for first in range(0, rows, TILE):
        part = pl.ds(first, TILE)
        raws = [ref[part, :].astype(jnp.float32) for ref in raw_refs]
        scales = row_scales(sum(jnp.sum(x * x, axis=-1, keepdims=True) for x in raws))
        accs = []
        for k in range(chunks):
            features = feature_slice(place, k, width)
            accs.append(acc_ref[part, features] + add_ref[part, features].astype(jnp.float32))
        units = [x * scales for x in raws]
        inner = sum(jnp.sum(u * a, axis=-1, keepdims=True) for u, a in zip(units, accs))
        for k in range(chunks):
            out_refs[k][part, :] = (scales * (accs[k] - units[k] * inner)).astype(jnp.bfloat16)


def place_text_body(chunks, *refs):
    where_ref, part_refs, out_ref = refs[0], refs[1 : 1 + chunks], refs[1 + chunks]
    place = where_ref[1]
    rows = part_refs[0].shape[0]
    for k in range(chunks):
        block = pl.ds(pl.multiple_of((place ^ k) * rows, rows), rows)
        out_ref[block, :] = part_refs[k][...]


def image_grad_body(sum_count, raw_ref, *refs):
    sum_refs, piece_refs, out_ref = refs[:sum_count], refs[sum_count:-1], refs[-1]
    step = 64
    for first in range(0, raw_ref.shape[0], step):
        part = pl.ds(first, step)
        raw = raw_ref[part, :].astype(jnp.float32)
        scales = row_scales(jnp.sum(raw * raw, axis=-1, keepdims=True))
        unit = raw * scales
        acc = sum(ref[part, :].astype(jnp.float32) for ref in sum_refs)
        if piece_refs:
            size = piece_refs[0].shape[0]
            acc += piece_refs[first // size][pl.ds(first % size, step), :].astype(jnp.float32)
        inner = jnp.sum(unit * acc, axis=-1, keepdims=True)
        out_ref[part, :] = (scales * (acc - unit * inner)).astype(jnp.bfloat16)


def swap(value, axis, bits):
    count = lax.axis_size(axis)
    return lax.ppermute(value, axis, [(i, i ^ bits) for i in range(count)])


def swap_near(value, which):
    count = lax.axis_size("blk")
    return lax.ppermute(value, "blk", [(i, i ^ neighbour_bits(i)[which]) for i in range(count)])


def per_device(text_emb, image_emb, logit_scale, logit_bias, bucket, positive, blocks):
    groups = lax.axis_size("tp")
    shards = lax.axis_size("blk")
    rows, embed = image_emb.shape
    tiles = rows // TILE
    width = text_emb.shape[1]
    where = jnp.stack([lax.axis_index("blk"), lax.axis_index("tp")]).astype(jnp.int32)
    square = shards == 4 * CORES

    def bf16(count, columns=embed):
        return struct((count, columns), jnp.bfloat16)

    def f32(count, columns=embed):
        return struct((count, columns), jnp.float32)

    if square:
        from_second = swap_near(image_emb, 1)
        from_first = swap_near(image_emb, 0)
    else:
        chips = shards // CORES
        same_core = [[chip * CORES + core for chip in range(chips)] for core in range(CORES)]
        gathered = lax.all_gather(
            image_emb, "blk", axis=0, tiled=True, axis_index_groups=same_core
        )
    picked = call_kernel(
        pick_body,
        [bf16(rows, width)] * groups,
        [where, text_emb],
        scalars=1,
        anywhere=(1,),
        scratch=[pltpu.SemaphoreType.DMA((groups,))],
        limit=60,
    )
    text_raw = [picked[0]] + [swap(picked[k], "tp", k) for k in range(1, groups)]
    if square:
        from_far = swap_near(from_second, 0)
        images = call_kernel(
            unit_images_body, [bf16(3 * rows)], [image_emb, from_first, from_second], limit=8
        )[0]
        text_raw[-1], images = lax.optimization_barrier((text_raw[-1], images))
    text_own, *pieces = call_kernel(
        functools.partial(unit_text_body, groups),
        [bf16(rows)] + [bf16(rows // TEXT_PIECES)] * TEXT_PIECES,
        [where] + text_raw,
        scalars=1,
        limit=8,
    )
    text_other = [swap(piece, "blk", 1) for piece in pieces]

    pair_operands = [
        logit_scale,
        logit_bias,
        where,
        blocks.transpose(2, 1, 0),
        bucket.reshape(-1, TILE),
        positive.reshape(-1, TILE),
    ]
    unit_flops = 2 * rows * rows * embed

    def pair_kernel(body, outs, operands, columns, products, scratch, limit, extra=()):
        return call_kernel(
            functools.partial(body, groups, tiles, *extra),
            outs,
            pair_operands + operands,
            scalars=4,
            scratch=scratch,
            flops=products * unit_flops,
            transcendentals=2 * rows * columns,
            limit=limit,
        )

    def finish_text(acc_own, acc_other):
        parts = call_kernel(
            functools.partial(text_grad_body, groups),
            [bf16(rows, width)] * groups,
            [where] + text_raw + [acc_own, swap(acc_other, "blk", 1)],
            scalars=1,
            limit=16,
        )
        return [parts[0]] + [swap(parts[k], "tp", k) for k in range(1, groups)]

    def place_text(text_parts):
        return call_kernel(
            functools.partial(place_text_body, groups),
            [bf16(groups * rows, width)],
            [where] + text_parts,
            scalars=1,
            flops=WAIT_FLOPS,
            limit=8,
        )[0]

    def finish_image(sums, pieces):
        return call_kernel(
            functools.partial(image_grad_body, len(sums)),
            [bf16(rows)],
            [image_emb] + sums + pieces,
            limit=8,
        )[0]

    if not square:
        columns = gathered.shape[0]
        spread, acc_own, acc_other = pair_kernel(
            all_body,
            [bf16(columns), f32(rows), bf16(rows)],
            [text_own, jnp.concatenate(text_other), gathered],
            2 * columns,
            6 * chips,
            [pltpu.VMEM((columns, embed), jnp.bfloat16), pltpu.VMEM((2 * rows, columns), jnp.bfloat16)],
            56,
            (chips,),
        )
        text_parts = finish_text(acc_own, acc_other)
        parts = lax.all_to_all(
            spread, "blk", split_axis=0, concat_axis=0, tiled=True, axis_index_groups=same_core
        )
        total = jnp.sum(parts.reshape(-1, rows, embed).astype(jnp.float32), axis=0)
        return (place_text(text_parts), finish_image([total], []))

    near_scratch = [pltpu.VMEM((rows, 3 * rows), jnp.bfloat16)]
    first_sum, second_sum, acc_own, own_weights = pair_kernel(
        near_own_body,
        [f32(rows), f32(rows), f32(rows), bf16(rows, rows)],
        [text_own, images],
        3 * rows,
        8,
        near_scratch,
        24,
    )
    text_other, first_sum, second_sum, acc_other, other_weights = pair_kernel(
        near_other_body,
        [bf16(rows), bf16(rows), f32(rows), f32(rows), bf16(rows, rows)],
        text_other + [images, first_sum, second_sum],
        3 * rows,
        8,
        near_scratch,
        24,
    )
    image_add = swap_near(first_sum, 0)
    acc_other, acc_own, far_sum = pair_kernel(
        far_body,
        [bf16(rows), f32(rows), bf16(rows)],
        [text_own, text_other, acc_own, acc_other, from_far],
        2 * rows,
        6,
        [pltpu.VMEM((rows, embed), jnp.bfloat16), pltpu.VMEM((rows, rows), jnp.bfloat16)],
        24,
    )
    image_add = call_kernel(widen_body, [f32(rows)], [image_add], limit=8)[0]
    acc_own, image_add = lax.optimization_barrier((acc_own, image_add))
    text_parts = finish_text(acc_own, acc_other)
    own_weights, text_parts[0] = lax.optimization_barrier((own_weights, text_parts[0]))
    base = call_kernel(
        own_sum_body,
        [f32(rows)],
        [own_weights, text_own, other_weights, text_other],
        flops=2 * unit_flops,
        limit=8,
    )[0]
    base, second_sum = lax.optimization_barrier((base, second_sum))
    far_in = swap_near(far_sum, 0)
    relayed = call_kernel(
        relay_body, [bf16(rows // LAST_PIECES)] * LAST_PIECES, [second_sum, far_in], limit=8
    )
    image_last = [swap_near(piece, 1) for piece in relayed]
    text_grad = place_text(text_parts)
    base, _ = lax.optimization_barrier((base, text_grad))
    return (text_grad, finish_image([base, image_add], image_last))


def solution(mesh):
    in_specs = (P("blk", "tp"), P(("blk", "tp"), None), P(), P(), P(), P(), P())
    out_specs = (P("blk", "tp"), P(("blk", "tp"), None))
    return jax.shard_map(
        per_device, mesh=mesh, in_specs=in_specs, out_specs=out_specs, check_vma=False
    )
```

time: 488 us -> 74.8 us (0.15)
  other arithmetic: 164 us -> 0.61 us
  local copies, waits for them, and re-layouts: 135 us -> 1.16 us
  matrix products: 107 us -> 0 us
  Pallas kernels: 0 us -> 22.7 us
  waiting for transfers between devices: 51.4 us -> 29.8 us
  between operations: 14.1 us -> 2.11 us
  starting transfers between devices: 11.2 us -> 18.2 us
    dot_general x16 -> x0, matrix products: 107 us -> none  [the longest x8 54.7 us: image_step(): jnp.einsum('cij,cid->cjd', weights, sender_text, preferred_element_type=j...]
    scatter-add x8 -> x0, other arithmetic: 98.4 us -> none  [image_step(): return image_acc.at[local_tile].add(update)]
    gather x57 -> x0, local copies, waits for them, and re-layouts: 47.5 us -> none  [the longest x8 19.1 us: image_step(): mine = image_tiles[local_tile]]
    all_to_all x2 -> x0, waiting for transfers between devices: 39.6 us -> none  [the longest x1 20.5 us: per_device(): lax.all_to_all(text_grad_local, 'tp', split_axis=1, concat_axis=0, tiled=...]
    ppermute x0 -> x15, waiting for transfers between devices: none -> 29.8 us  [the longest x6 16.7 us: swap_near(): lax.ppermute(value, 'blk', [(i, i ^ neighbour_bits(i)[which]) for i in ra...]
    reduce_sum x12 -> x0, other arithmetic: 28.9 us -> none  [the longest x8 24.9 us: text_step(): return text_acc + update.reshape(tile_count, SLOTS, TILE, width).sum(axis=1)]
    broadcast_in_dim x34 -> x0, local copies, waits for them, and re-layouts: 28.3 us -> none  [the longest x8 23.3 us: per_device(): text_repeat = jnp.repeat(text_tiles, SLOTS, axis=0)]
    pallas_call x0 -> x12, Pallas kernels: none -> 22.7 us  [call_kernel(): pl.pallas_call(body, out_shape=outs, in_specs=specs, out_specs=[VMEM_SPEC...]
  transfers between devices with their start and end apart: 4 -> 15, of which waited for: 3 -> 7; matrix products, arithmetic and copies ran while one was open for 36% -> 1% of each run, Pallas kernels for 0% -> 28%
where the time goes in v3:
time: 74.8 us; the launch traced here: 74.6 us
  waiting for transfers between devices  29.8 us (40%)
  Pallas kernels  22.7 us (30%)
  starting transfers between devices  18.2 us (24%)
  between operations  2.11 us (3%)
  local copies, waits for them, and re-layouts  1.16 us (2%)
    pallas_call x12, Pallas kernels, call_kernel(): pl.pallas_call(body, out_shape=outs, in_specs=specs, out_specs=[VMEM_SPEC...  22.7 us
    ppermute x6, waiting for transfers between devices, swap_near(): lax.ppermute(value, 'blk', [(i, i ^ neighbour_bits(i)[which]) for i in ra...  16.7 us
    ppermute x9, waiting for transfers between devices, swap(): return lax.ppermute(value, axis, [(i, i ^ bits) for i in range(count)])  13.1 us
    ppermute x9, starting transfers between devices, swap(): return lax.ppermute(value, axis, [(i, i ^ bits) for i in range(count)])  9.54 us
    ppermute x6, starting transfers between devices, swap_near(): lax.ppermute(value, 'blk', [(i, i ^ neighbour_bits(i)[which]) for i in ra...  8.65 us
  transfers between devices with their start and end apart: 15, of which 7 were waited for; matrix products, arithmetic and copies ran while one was open for 1% of the time, Pallas kernels for 28%

profile of v3, /device:TPU:0, one launch (start us, length us, event | category | flops | bytes accessed | tf_op | source)
XLA Modules:
  0.0 74.6 jit_solution(14116179848004850231)
XLA Ops:
  0.6 3.0 %collective-permute-start.4 = (bf16[384,1024]{1,0:T(8,128)(2,1)}, bf16[384,1024]{1,0:T(8,128)(2,1)S(1)}, u32[]{:S(2)}, u32[]{:S(2)}) collective-permute-start(bf16[384,1024]{1,0:T(8,128)(2,1)} %raw_ref.1), channel_id=1, source_target_pairs={{0,16},{4,12},{8,24},{12,4},{16,0},{20,28},{24,8},{28,20},{1,17},{... | collective-permute-start | bytes 2359304 | tf_op jit(solution)/shard_map/ppermute | solution.py:343
  3.7 1.5 %collective-permute-start.3 = (bf16[384,1024]{1,0:T(8,128)(2,1)}, bf16[384,1024]{1,0:T(8,128)(2,1)S(1)}, u32[]{:S(2)}, u32[]{:S(2)}) collective-permute-start(bf16[384,1024]{1,0:T(8,128)(2,1)} %raw_ref.1), channel_id=1, source_target_pairs={{0,8},{4,20},{8,0},{12,28},{16,24},{20,4},{24,16},{28,12},{1,9},{5... | collective-permute-start | bytes 2359304 | tf_op jit(solution)/shard_map/ppermute | solution.py:343
  5.2 0.6 pad_add_fusion.where_ref.refs_0_.refs_2_
  5.8 2.8 %shard_map.86 = (bf16[384,256]{1,0:T(8,128)(2,1)}, bf16[384,256]{1,0:T(8,128)(2,1)}, bf16[384,256]{1,0:T(8,128)(2,1)}, bf16[384,256]{1,0:T(8,128)(2,1)}) custom-call(s32[2]{0:T(128)} %pad_add_fusion.where_ref.refs_0_.refs_2_, bf16[1536,256]{1,0:T(8,128)(2,1)} %text_ref.1), custom_call_target="tpu_custom_call" | custom-call | bytes 1572872 | tf_op jit(solution)/shard_map/pallas_call | solution.py:33
  8.6 3.7 %collective-permute-start.2 = (bf16[384,256]{1,0:T(8,128)(2,1)}, bf16[384,256]{1,0:T(8,128)(2,1)S(1)}, u32[]{:S(2)}, u32[]{:S(2)}) collective-permute-start(bf16[384,256]{1,0:T(8,128)(2,1)} %get-tuple-element.37), channel_id=1, source_target_pairs={{0,3},{1,2},{2,1},{3,0},{4,7},{5,6},{6,5},{7,4},{8,11},{9,10},{10,... | collective-permute-start | bytes 589832 | tf_op jit(solution)/shard_map/ppermute | solution.py:338
  12.2 0.0 collective-permute-start
  12.2 0.8 %collective-permute-start.1 = (bf16[384,256]{1,0:T(8,128)(2,1)}, bf16[384,256]{1,0:T(8,128)(2,1)S(1)}, u32[]{:S(2)}, u32[]{:S(2)}) collective-permute-start(bf16[384,256]{1,0:T(8,128)(2,1)} %get-tuple-element.36), channel_id=1, source_target_pairs={{0,2},{1,3},{2,0},{3,1},{4,6},{5,7},{6,4},{7,5},{8,10},{9,11},{10,... | collective-permute-start | bytes 589832 | tf_op jit(solution)/shard_map/ppermute | solution.py:338
  13.0 8.8 %collective-permute-done.4.refs_2_ = bf16[384,1024]{1,0:T(8,128)(2,1)S(1)} collective-permute-done((bf16[384,1024]{1,0:T(8,128)(2,1)}, bf16[384,1024]{1,0:T(8,128)(2,1)S(1)}, u32[]{:S(2)}, u32[]{:S(2)}) %collective-permute-start.4) | collective-permute-done | bytes 786464 | tf_op jit(solution)/shard_map/ppermute | solution.py:343
  21.8 1.4 %collective-permute-start.7 = (bf16[384,1024]{1,0:T(8,128)(2,1)S(1)}, bf16[384,1024]{1,0:T(8,128)(2,1)S(1)}, u32[]{:S(2)}, u32[]{:S(2)}) collective-permute-start(bf16[384,1024]{1,0:T(8,128)(2,1)S(1)} %collective-permute-done.4.refs_2_), channel_id=1, source_target_pairs={{0,8},{4,20},{8,0},{12,28},{16,24},{20,4},{24,16},{28,12},{1,9},{5... | collective-permute-start | bytes 2359304 | tf_op jit(solution)/shard_map/ppermute | solution.py:343
  23.2 0.0 collective-permute-done.3.refs_1_
  23.2 1.1 %copy-done = bf16[384,1024]{1,0:T(8,128)(2,1)S(1)} copy-done((bf16[384,1024]{1,0:T(8,128)(2,1)S(1)}, bf16[384,1024]{1,0:T(8,128)(2,1)}, u32[]{:S(2)}) %copy-start) | copy-done | bytes 786456
  24.4 0.7 shard_map.87.refs_7_.refs_8_
  25.1 0.0 collective-permute-done.2.refs_4_
  25.1 0.0 collective-permute-done.refs_2_
  25.1 3.4 %collective-permute-done.1.refs_3_ = bf16[384,256]{1,0:T(8,128)(2,1)S(1)} collective-permute-done((bf16[384,256]{1,0:T(8,128)(2,1)}, bf16[384,256]{1,0:T(8,128)(2,1)S(1)}, u32[]{:S(2)}, u32[]{:S(2)}) %collective-permute-start.1) | collective-permute-done | bytes 196640 | tf_op jit(solution)/shard_map/ppermute | solution.py:338
  28.6 0.0 copy-done.3
  28.6 0.9 %shard_map.88 = (bf16[384,1024]{1,0:T(8,128)(2,1)S(1)}, bf16[192,1024]{1,0:T(8,128)(2,1)S(1)}, bf16[192,1024]{1,0:T(8,128)(2,1)S(1)}) custom-call(s32[2]{0:T(128)S(1)} %copy-done.3, bf16[384,256]{1,0:T(8,128)(2,1)S(1)} %copy-done.2, bf16[384,256]{1,0:T(8,128)(2,1)S(1)} %collective-permute-done.refs_2_, bf16[384,256]{1,0:T(8,128)(2,1)S(1)} %collective-permute-done.1.refs_3_, ...), custom_call_target="tpu_custom_call" | custom-call | bytes 2359304 | tf_op jit(solution)/shard_map/pallas_call | solution.py:33
  29.5 0.1 collective-permute-start.5
  29.6 0.5 collective-permute-start.6
  31.4 0.0 copy-done.4
  31.4 0.0 copy-done.5
  31.4 4.4 %shard_map.89 = (f32[384,1024]{1,0:T(8,128)S(1)}, f32[384,1024]{1,0:T(8,128)S(1)}, f32[384,1024]{1,0:T(8,128)S(1)}, bf16[384,384]{1,0:T(8,128)(2,1)S(1)}) custom-call(f32[1]{0:T(128)S(6)} %copy.9.refs_0_, f32[1]{0:T(128)S(6)} %copy.10.refs_1_, s32[2]{0:T(128)S(1)} %copy-done.3, s32[3,8,96]{2,1,0:T(8,128)S(1)} %bitcast.11, s32[96,128]{1,0:T(8,128)S(1)} %bitcast.5, ...), custom_call_target="tpu_custom_call" | custom-call | flops 2415919104 | bytes 8266768 | tf_op jit(solution)/shard_map/pallas_call | solution.py:33
  35.8 0.0 collective-permute-done.5.refs_6_
  35.8 0.0 collective-permute-done.6.refs_7_
  35.8 4.5 %shard_map.90 = (bf16[384,1024]{1,0:T(8,128)(2,1)S(1)}, bf16[384,1024]{1,0:T(8,128)(2,1)S(1)}, f32[384,1024]{1,0:T(8,128)S(1)}, f32[384,1024]{1,0:T(8,128)S(1)}, bf16[384,384]{1,0:T(8,128)(2,1)S(1)}) custom-call(f32[1]{0:T(128)S(6)} %copy.9.refs_0_, f32[1]{0:T(128)S(6)} %copy.10.refs_1_, s32[2]{0:T(128)S(1)} %copy-done.3, s32[3,8,96]{2,1,0:T(8,128)S(1)} %bitcast.12, ...), custom_call_target="tpu_custom_call" | custom-call | flops 2415919104 | bytes 11412496 | tf_op jit(solution)/shard_map/pallas_call | solution.py:33
  40.3 0.6 collective-permute-start.8
  40.9 0.0 collective-permute-done.7.refs_10_
  40.9 3.8 %shard_map.91 = (bf16[384,1024]{1,0:T(8,128)(2,1)S(1)}, f32[384,1024]{1,0:T(8,128)S(1)}, bf16[384,1024]{1,0:T(8,128)(2,1)S(1)}) custom-call(f32[1]{0:T(128)S(6)} %copy.9.refs_0_, f32[1]{0:T(128)S(6)} %copy.10.refs_1_, s32[2]{0:T(128)S(1)} %copy-done.3, s32[3,8,96]{2,1,0:T(8,128)S(1)} %bitcast.13, s32[96,128]{1,0:T(8,128)S(1)} %bitcast.7, ...), custom_call_target="tpu_custom_call" | custom-call | flops 1811939328 | bytes 8758288 | tf_op jit(solution)/shard_map/pallas_call | solution.py:33
  44.7 0.1 collective-permute-start.9
  44.8 1.6 %collective-permute-start.13 = (bf16[384,1024]{1,0:T(8,128)(2,1)S(1)}, bf16[384,1024]{1,0:T(8,128)(2,1)S(1)}, u32[]{:S(2)}, u32[]{:S(2)}) collective-permute-start(bf16[384,1024]{1,0:T(8,128)(2,1)S(1)} %get-tuple-element.65), channel_id=1, source_target_pairs={{0,8},{4,20},{8,0},{12,28},{16,24},{20,4},{24,16},{28,12},{1,9},{5... | collective-permute-start | bytes 2359304 | tf_op jit(solution)/shard_map/ppermute | solution.py:343
  46.3 6.0 %collective-permute-done.8.in_ref = bf16[384,1024]{1,0:T(8,128)(2,1)S(1)} collective-permute-done((bf16[384,1024]{1,0:T(8,128)(2,1)S(1)}, bf16[384,1024]{1,0:T(8,128)(2,1)S(1)}, u32[]{:S(2)}, u32[]{:S(2)}) %collective-permute-start.8) | collective-permute-done | bytes 786464 | tf_op jit(solution)/shard_map/ppermute | solution.py:343
  52.3 0.1 shard_map.92.refs_1_
  52.4 0.0 collective-permute-done.9.refs_6_
  52.5 1.3 %shard_map.93 = (bf16[384,256]{1,0:T(8,128)(2,1)S(1)}, bf16[384,256]{1,0:T(8,128)(2,1)S(1)}, bf16[384,256]{1,0:T(8,128)(2,1)S(1)}, bf16[384,256]{1,0:T(8,128)(2,1)S(1)}) custom-call(s32[2]{0:T(128)S(1)} %copy-done.3, bf16[384,256]{1,0:T(8,128)(2,1)S(1)} %copy-done.2, bf16[384,256]{1,0:T(8,128)(2,1)S(1)} %collective-permute-done.refs_2_, ...), custom_call_target="tpu_custom_call" | custom-call | bytes 3932168 | tf_op jit(solution)/shard_map/pallas_call | solution.py:33
  53.8 0.1 collective-permute-start.10
  53.9 3.0 %collective-permute-start.11 = (bf16[384,256]{1,0:T(8,128)(2,1)S(1)}, bf16[384,256]{1,0:T(8,128)(2,1)S(1)}, u32[]{:S(2)}, u32[]{:S(2)}) collective-permute-start(bf16[384,256]{1,0:T(8,128)(2,1)S(1)} %get-tuple-element.56), channel_id=1, source_target_pairs={{0,2},{1,3},{2,0},{3,1},{4,6},{5,7},{6,4},{7,5},{8,10},{9,11},{10,... | collective-permute-start | bytes 589832 | tf_op jit(solution)/shard_map/ppermute | solution.py:338
  56.9 1.3 %collective-permute-start.12 = (bf16[384,256]{1,0:T(8,128)(2,1)S(1)}, bf16[384,256]{1,0:T(8,128)(2,1)S(1)}, u32[]{:S(2)}, u32[]{:S(2)}) collective-permute-start(bf16[384,256]{1,0:T(8,128)(2,1)S(1)} %get-tuple-element.57), channel_id=1, source_target_pairs={{0,3},{1,2},{2,1},{3,0},{4,7},{5,6},{6,5},{7,4},{8,11},{9,10},{10,... | collective-permute-start | bytes 589832 | tf_op jit(solution)/shard_map/ppermute | solution.py:338
  58.3 1.0 %shard_map.95.refs_0_ = f32[384,1024]{1,0:T(8,128)S(1)} custom-call(bf16[384,384]{1,0:T(8,128)(2,1)S(1)} %get-tuple-element.58.own_weight_ref, bf16[384,1024]{1,0:T(8,128)(2,1)S(1)} %get-tuple-element.39.refs_6_.own_ref, bf16[384,384]{1,0:T(8,128)(2,1)S(1)} %get-tuple-element.59.other_weight_ref, bf16[384,1024]{1,0:T(8,128)(2,1)S(1)} %get-tuple-element.46.refs_7_.other_ref), custom_call_target="tpu_custom_call" | custom-call | flops 603979776 | bytes 3735552 | tf_op jit(solution)/shard_map/pallas_call | solution.py:33
  59.3 1.5 %collective-permute-done.13.in_ref = bf16[384,1024]{1,0:T(8,128)(2,1)S(1)} collective-permute-done((bf16[384,1024]{1,0:T(8,128)(2,1)S(1)}, bf16[384,1024]{1,0:T(8,128)(2,1)S(1)}, u32[]{:S(2)}, u32[]{:S(2)}) %collective-permute-start.13) | collective-permute-done | bytes 786464 | tf_op jit(solution)/shard_map/ppermute | solution.py:343
  60.8 0.1 shard_map.96
  60.9 0.0 copy-start.1
  60.9 0.6 collective-permute-start.14
  61.5 1.6 %collective-permute-done.10.refs_2_ = bf16[384,256]{1,0:T(8,128)(2,1)S(1)} collective-permute-done((bf16[384,256]{1,0:T(8,128)(2,1)S(1)}, bf16[384,256]{1,0:T(8,128)(2,1)S(1)}, u32[]{:S(2)}, u32[]{:S(2)}) %collective-permute-start.10) | collective-permute-done | bytes 196640 | tf_op jit(solution)/shard_map/ppermute | solution.py:338
  63.1 8.0 %collective-permute-done.11.refs_3_ = bf16[384,256]{1,0:T(8,128)(2,1)S(1)} collective-permute-done((bf16[384,256]{1,0:T(8,128)(2,1)S(1)}, bf16[384,256]{1,0:T(8,128)(2,1)S(1)}, u32[]{:S(2)}, u32[]{:S(2)}) %collective-permute-start.11) | collective-permute-done | bytes 196640 | tf_op jit(solution)/shard_map/ppermute | solution.py:338
  71.2 0.0 collective-permute-done.12.refs_4_
  71.2 1.5 %shard_map.94 = bf16[1536,256]{1,0:T(8,128)(2,1)} custom-call(s32[2]{0:T(128)S(1)} %copy-done.3, bf16[384,256]{1,0:T(8,128)(2,1)S(1)} %get-tuple-element.54.refs_1_, bf16[384,256]{1,0:T(8,128)(2,1)S(1)} %collective-permute-done.10.refs_2_, bf16[384,256]{1,0:T(8,128)(2,1)S(1)} %collective-permute-done.11.refs_3_, ...), custom_call_target="tpu_custom_call" | custom-call | flops 20000000000 | bytes 1572872 | tf_op jit(solution)/shard_map/pallas_call | solution.py:33
  72.6 0.3 collective-permute-done.14.refs_2_
  73.0 1.6 %shard_map.97 = bf16[384,1024]{1,0:T(8,128)(2,1)} custom-call(bf16[384,1024]{1,0:T(8,128)(2,1)S(1)} %copy-done.1, f32[384,1024]{1,0:T(8,128)S(1)} %shard_map.95.refs_0_, f32[384,1024]{1,0:T(8,128)S(1)} %shard_map.92.refs_1_, bf16[384,1024]{1,0:T(8,128)(2,1)S(1)} %collective-permute-done.14.refs_2_), custom_call_target="tpu_custom_call" | custom-call | bytes 5505024 | tf_op jit(solution)/shard_map/pallas_call | solution.py:33
  (9 shorter events, 0.0 us)
Async XLA Ops:
  0.6 21.2 %collective-permute-start.4 = (bf16[384,1024]{1,0:T(8,128)(2,1)}, bf16[384,1024]{1,0:T(8,128)(2,1)S(1)}, u32[]{:S(2)}, u32[]{:S(2)}) collective-permute-start(bf16[384,1024]{1,0:T(8,128)(2,1)} %raw_ref.1), channel_id=1, source_target_pairs={{0,16},{4,12},{8,24},{12,4},{16,0},{20,28},{24,8},{28,20},{1,17},{... | collective-permute-start | bytes 2359304 | tf_op jit(solution)/shard_map/ppermute | solution.py:343
  3.7 19.6 %collective-permute-start.3 = (bf16[384,1024]{1,0:T(8,128)(2,1)}, bf16[384,1024]{1,0:T(8,128)(2,1)S(1)}, u32[]{:S(2)}, u32[]{:S(2)}) collective-permute-start(bf16[384,1024]{1,0:T(8,128)(2,1)} %raw_ref.1), channel_id=1, source_target_pairs={{0,8},{4,20},{8,0},{12,28},{16,24},{20,4},{24,16},{28,12},{1,9},{5... | collective-permute-start | bytes 2359304 | tf_op jit(solution)/shard_map/ppermute | solution.py:343
  8.6 16.6 %collective-permute-start.2 = (bf16[384,256]{1,0:T(8,128)(2,1)}, bf16[384,256]{1,0:T(8,128)(2,1)S(1)}, u32[]{:S(2)}, u32[]{:S(2)}) collective-permute-start(bf16[384,256]{1,0:T(8,128)(2,1)} %get-tuple-element.37), channel_id=1, source_target_pairs={{0,3},{1,2},{2,1},{3,0},{4,7},{5,6},{6,5},{7,4},{8,11},{9,10},{10,... | collective-permute-start | bytes 589832 | tf_op jit(solution)/shard_map/ppermute | solution.py:338
  12.2 12.9 %collective-permute-start = (bf16[384,256]{1,0:T(8,128)(2,1)}, bf16[384,256]{1,0:T(8,128)(2,1)S(1)}, u32[]{:S(2)}, u32[]{:S(2)}) collective-permute-start(bf16[384,256]{1,0:T(8,128)(2,1)} %get-tuple-element.35), channel_id=1, source_target_pairs={{0,1},{1,0},{2,3},{3,2},{4,5},{5,4},{6,7},{7,6},{8,9},{9,8},{10,11... | collective-permute-start | bytes 589832 | tf_op jit(solution)/shard_map/ppermute | solution.py:338
  12.2 16.3 %copy-start.3 = (s32[2]{0:T(128)S(1)}, s32[2]{0:T(128)}, u32[]{:S(2)}) copy-start(s32[2]{0:T(128)} %pad_add_fusion.where_ref.refs_0_.refs_2_) | copy-start | bytes 28
  12.2 16.3 %collective-permute-start.1 = (bf16[384,256]{1,0:T(8,128)(2,1)}, bf16[384,256]{1,0:T(8,128)(2,1)S(1)}, u32[]{:S(2)}, u32[]{:S(2)}) collective-permute-start(bf16[384,256]{1,0:T(8,128)(2,1)} %get-tuple-element.36), channel_id=1, source_target_pairs={{0,2},{1,3},{2,0},{3,1},{4,6},{5,7},{6,4},{7,5},{8,10},{9,11},{10,... | collective-permute-start | bytes 589832 | tf_op jit(solution)/shard_map/ppermute | solution.py:338
  21.8 19.1 %collective-permute-start.7 = (bf16[384,1024]{1,0:T(8,128)(2,1)S(1)}, bf16[384,1024]{1,0:T(8,128)(2,1)S(1)}, u32[]{:S(2)}, u32[]{:S(2)}) collective-permute-start(bf16[384,1024]{1,0:T(8,128)(2,1)S(1)} %collective-permute-done.4.refs_2_), channel_id=1, source_target_pairs={{0,8},{4,20},{8,0},{12,28},{16,24},{20,4},{24,16},{28,12},{1,9},{5... | collective-permute-start | bytes 2359304 | tf_op jit(solution)/shard_map/ppermute | solution.py:343
  23.2 1.1 %copy-start = (bf16[384,1024]{1,0:T(8,128)(2,1)S(1)}, bf16[384,1024]{1,0:T(8,128)(2,1)}, u32[]{:S(2)}) copy-start(bf16[384,1024]{1,0:T(8,128)(2,1)} %raw_ref.1) | copy-start | bytes 2359300
  24.4 4.2 %copy-start.2 = (bf16[384,256]{1,0:T(8,128)(2,1)S(1)}, bf16[384,256]{1,0:T(8,128)(2,1)}, u32[]{:S(2)}) copy-start(bf16[384,256]{1,0:T(8,128)(2,1)} %get-tuple-element.34.refs_1_) | copy-start | bytes 589828
  24.4 7.0 %copy-start.4 = (s32[12288]{0:T(1024)S(1)}, s32[12288]{0:T(1024)}, u32[]{:S(2)}) copy-start(s32[12288]{0:T(1024)} %param.11) | copy-start | bytes 147460
  24.4 7.0 %copy-start.5 = (s32[12288]{0:T(1024)S(1)}, s32[12288]{0:T(1024)}, u32[]{:S(2)}) copy-start(s32[12288]{0:T(1024)} %param.12) | copy-start | bytes 147460
  24.4 7.0 %copy-start.6 = (s32[96,8,3]{0,1,2:T(8,128)S(1)}, s32[96,8,3]{0,1,2:T(8,128)}, u32[]{:S(2)}) copy-start(s32[96,8,3]{0,1,2:T(8,128)} %param.13) | copy-start | bytes 27652
  29.5 6.3 %collective-permute-start.5 = (bf16[192,1024]{1,0:T(8,128)(2,1)S(1)}, bf16[192,1024]{1,0:T(8,128)(2,1)S(1)}, u32[]{:S(2)}, u32[]{:S(2)}) collective-permute-start(bf16[192,1024]{1,0:T(8,128)(2,1)S(1)} %get-tuple-element.42), channel_id=1, source_target_pairs={{0,4},{4,0},{8,12},{12,8},{16,20},{20,16},{24,28},{28,24},{1,5},{5... | collective-permute-start | bytes 1179656 | tf_op jit(solution)/shard_map/ppermute | solution.py:338
  29.6 6.2 %collective-permute-start.6 = (bf16[192,1024]{1,0:T(8,128)(2,1)S(1)}, bf16[192,1024]{1,0:T(8,128)(2,1)S(1)}, u32[]{:S(2)}, u32[]{:S(2)}) collective-permute-start(bf16[192,1024]{1,0:T(8,128)(2,1)S(1)} %get-tuple-element.43), channel_id=1, source_target_pairs={{0,4},{4,0},{8,12},{12,8},{16,20},{20,16},{24,28},{28,24},{1,5},{5... | collective-permute-start | bytes 1179656 | tf_op jit(solution)/shard_map/ppermute | solution.py:338
  40.3 12.1 %collective-permute-start.8 = (bf16[384,1024]{1,0:T(8,128)(2,1)S(1)}, bf16[384,1024]{1,0:T(8,128)(2,1)S(1)}, u32[]{:S(2)}, u32[]{:S(2)}) collective-permute-start(bf16[384,1024]{1,0:T(8,128)(2,1)S(1)} %get-tuple-element.50), channel_id=1, source_target_pairs={{0,8},{4,20},{8,0},{12,28},{16,24},{20,4},{24,16},{28,12},{1,9},{5... | collective-permute-start | bytes 2359304 | tf_op jit(solution)/shard_map/ppermute | solution.py:343
  44.7 7.8 %collective-permute-start.9 = (bf16[384,1024]{1,0:T(8,128)(2,1)S(1)}, bf16[384,1024]{1,0:T(8,128)(2,1)S(1)}, u32[]{:S(2)}, u32[]{:S(2)}) collective-permute-start(bf16[384,1024]{1,0:T(8,128)(2,1)S(1)} %get-tuple-element.52), channel_id=1, source_target_pairs={{0,4},{4,0},{8,12},{12,8},{16,20},{20,16},{24,28},{28,24},{1,5},{5... | collective-permute-start | bytes 2359304 | tf_op jit(solution)/shard_map/ppermute | solution.py:338
  44.8 16.0 %collective-permute-start.13 = (bf16[384,1024]{1,0:T(8,128)(2,1)S(1)}, bf16[384,1024]{1,0:T(8,128)(2,1)S(1)}, u32[]{:S(2)}, u32[]{:S(2)}) collective-permute-start(bf16[384,1024]{1,0:T(8,128)(2,1)S(1)} %get-tuple-element.65), channel_id=1, source_target_pairs={{0,8},{4,20},{8,0},{12,28},{16,24},{20,4},{24,16},{28,12},{1,9},{5... | collective-permute-start | bytes 2359304 | tf_op jit(solution)/shard_map/ppermute | solution.py:343
  53.8 9.3 %collective-permute-start.10 = (bf16[384,256]{1,0:T(8,128)(2,1)S(1)}, bf16[384,256]{1,0:T(8,128)(2,1)S(1)}, u32[]{:S(2)}, u32[]{:S(2)}) collective-permute-start(bf16[384,256]{1,0:T(8,128)(2,1)S(1)} %get-tuple-element.55), channel_id=1, source_target_pairs={{0,1},{1,0},{2,3},{3,2},{4,5},{5,4},{6,7},{7,6},{8,9},{9,8},{10,11... | collective-permute-start | bytes 589832 | tf_op jit(solution)/shard_map/ppermute | solution.py:338
  53.9 17.3 %collective-permute-start.11 = (bf16[384,256]{1,0:T(8,128)(2,1)S(1)}, bf16[384,256]{1,0:T(8,128)(2,1)S(1)}, u32[]{:S(2)}, u32[]{:S(2)}) collective-permute-start(bf16[384,256]{1,0:T(8,128)(2,1)S(1)} %get-tuple-element.56), channel_id=1, source_target_pairs={{0,2},{1,3},{2,0},{3,1},{4,6},{5,7},{6,4},{7,5},{8,10},{9,11},{10,... | collective-permute-start | bytes 589832 | tf_op jit(solution)/shard_map/ppermute | solution.py:338
  56.9 14.2 %collective-permute-start.12 = (bf16[384,256]{1,0:T(8,128)(2,1)S(1)}, bf16[384,256]{1,0:T(8,128)(2,1)S(1)}, u32[]{:S(2)}, u32[]{:S(2)}) collective-permute-start(bf16[384,256]{1,0:T(8,128)(2,1)S(1)} %get-tuple-element.57), channel_id=1, source_target_pairs={{0,3},{1,2},{2,1},{3,0},{4,7},{5,6},{6,5},{7,4},{8,11},{9,10},{10,... | collective-permute-start | bytes 589832 | tf_op jit(solution)/shard_map/ppermute | solution.py:338
  60.9 12.1 %copy-start.1 = (bf16[384,1024]{1,0:T(8,128)(2,1)S(1)}, bf16[384,1024]{1,0:T(8,128)(2,1)}, u32[]{:S(2)}) copy-start(bf16[384,1024]{1,0:T(8,128)(2,1)} %raw_ref.1) | copy-start | bytes 2359300
  60.9 12.1 %collective-permute-start.14 = (bf16[384,1024]{1,0:T(8,128)(2,1)S(1)}, bf16[384,1024]{1,0:T(8,128)(2,1)S(1)}, u32[]{:S(2)}, u32[]{:S(2)}) collective-permute-start(bf16[384,1024]{1,0:T(8,128)(2,1)S(1)} %shard_map.96), channel_id=1, source_target_pairs={{0,16},{4,12},{8,24},{12,4},{16,0},{20,28},{24,8},{28,20},{1,17},{... | collective-permute-start | bytes 2359304 | tf_op jit(solution)/shard_map/ppermute | solution.py:343
